TPU v7x, 32 devices: a whole 2x2x4 slice. The times are simulated.
32 devices in a mesh: gy: 8 (over z, x), gz: 4 (over y, core).
Axes of the slice: x: 2, y: 2, z: 4, core: 2. Of those that a mesh axis runs over, the one named last changes fastest.
Arguments:
- heat_scalar_window: float32 [128, 32, 2048], P('gy', 'gz'), may hold values from -6 to 6
- flow_speed_vector: bfloat16 [3, 128, 32, 2048], P(None, 'gy', 'gz'), may hold values from -4 to 4
Outputs:
- updated: float32 [128, 32, 2048], P('gy', 'gz')
All inputs are finite; a program needn't handle non-finite values.
Results may differ from a plain program's by a relative error of at most 0.0003.
Values sent between devices are 32-bit elements; how exact they have to be, the bound alone decides.
A program may use at most 64 MiB of HBM per device.

v0:
```python
import jax
import jax.numpy as jnp
from jax import lax
from jax.sharding import PartitionSpec as P

XB = 128
RX = 1
RY = 768
RZ = 192


EXACT = lax.Precision.HIGHEST
thermal_conduction_coefficient = 0.15


def extended(cells, sides, width):
    for axis, dim in sides:
        count = lax.axis_size(axis)
        ends = count - 1
        head = lax.slice_in_dim(cells, 0, width, axis=dim)
        tail = lax.slice_in_dim(cells, cells.shape[dim] - width, cells.shape[dim], axis=dim)
        cells = jnp.concatenate(
            [
                lax.ppermute(tail, axis, [(i, (i + 1) % count) for i in range(ends)]),
                cells,
                lax.ppermute(head, axis, [((i + 1) % count, i) for i in range(ends)]),
            ],
            axis=dim,
        )
    return cells


def prefix(value, axis, join, neutral, backward):
    count, mine = (lax.axis_size(axis), lax.axis_index(axis))
    pieces = jax.tree.map(lambda part: lax.all_gather(part, axis), value)
    if backward:
        pieces = jax.tree.map(lambda part: part[::-1], pieces)
        mine = count - 1 - mine
    so_far = jax.tree.map(
        lambda part, zero: jnp.full_like(part, 0) + jnp.asarray(zero, part.dtype), value, neutral
    )

    def hop(position, so_far):
        longer = join(so_far, jax.tree.map(lambda part: part[position], pieces))
        return jax.tree.map(lambda new, old: jnp.where(position < mine, new, old), longer, so_far)

    return lax.fori_loop(0, count - 1, hop, so_far)


def line_inverse(line_count, ratio_value):
    coupling = jnp.float32(ratio_value)
    half_step = 0.5 / coupling
    decay_base = 1.0 + half_step - jnp.sqrt(half_step * (2.0 + half_step))
    places = jnp.arange(line_count, dtype=jnp.float32)
    small_index = jnp.minimum(places[:, None], places[None, :])
    large_index = jnp.maximum(places[:, None], places[None, :])
    span_value = jnp.float32(line_count)
    numer = (
        decay_base ** (large_index - small_index + 1.0)
        * (1.0 - decay_base ** (2.0 * (small_index + 1.0)))
        * (1.0 - decay_base ** (2.0 * (span_value - large_index)))
    )
    denom = (
        coupling * (1.0 - decay_base * decay_base) * (1.0 - decay_base ** (2.0 * span_value + 2.0))
    )
    return numer / denom


def product_two(left_two, right_two):
    return jnp.sum(left_two[:, :, None] * right_two[None, :, :], axis=1)


def apply_two(matrix, vector):
    return jnp.stack(
        [
            matrix[0, 0] * vector[0] + matrix[0, 1] * vector[1],
            matrix[1, 0] * vector[0] + matrix[1, 1] * vector[1],
        ]
    )


def inverse_two(matrix):
    determinant = matrix[0, 0] * matrix[1, 1] - matrix[0, 1] * matrix[1, 0]
    return (
        jnp.stack(
            [jnp.stack([matrix[1, 1], -matrix[0, 1]]), jnp.stack([-matrix[1, 0], matrix[0, 0]])]
        )
        / determinant
    )


def couplers(inverse_block, ratio_value):
    near_value = ratio_value * inverse_block[0, 0]
    far_value = ratio_value * inverse_block[0, -1]
    zero_value = jnp.zeros_like(near_value)
    lower_map = jnp.stack([jnp.stack([zero_value, near_value]), jnp.stack([zero_value, far_value])])
    upper_map = jnp.stack([jnp.stack([far_value, zero_value]), jnp.stack([near_value, zero_value])])
    return (lower_map, upper_map)


def reduced_factors(lower_map, upper_map, line_count):
    unit_two = jnp.eye(2, dtype=jnp.float32)

    def advance(earlier_value, ignored):
        following = inverse_two(
            unit_two - product_two(product_two(lower_map, earlier_value), upper_map)
        )
        return (following, following)

    final_value, remaining = lax.scan(advance, unit_two, None, length=line_count - 1)
    return jnp.concatenate([unit_two[None], remaining], axis=0)


def solve_chain(stacked, dinvs, lower_map, upper_map):

    def forward(earlier_value, inputs):
        source_value, factor_prior = inputs
        following = source_value + apply_two(product_two(lower_map, factor_prior), earlier_value)
        return (following, following)

    first_value = stacked[0]
    final_value, remaining = lax.scan(forward, first_value, (stacked[1:], dinvs[:-1]))
    swept = jnp.concatenate([first_value[None], remaining], axis=0)
    end_value = apply_two(dinvs[-1], swept[-1])

    def backward(after_value, inputs):
        swept_value, factor_here = inputs
        current = apply_two(factor_here, swept_value + apply_two(upper_map, after_value))
        return (current, current)

    unused_top, lower_values = lax.scan(backward, end_value, (swept[:-1], dinvs[:-1]), reverse=True)
    solved = jnp.concatenate([lower_values, end_value[None]], axis=0)
    blank_row = jnp.zeros_like(solved[:1, 0])
    before_value = jnp.concatenate([blank_row, solved[:-1, 1]], axis=0)
    after_value = jnp.concatenate([solved[1:, 0], blank_row], axis=0)
    return jnp.stack([before_value, after_value], axis=1)


def compose(earlier, later_map):
    return (
        product_two(later_map[0], earlier[0]),
        apply_two(later_map[0], earlier[1]) + later_map[1],
    )


def on_device(heat_scalar_window, flow_speed_vector):
    haloed_array = extended(heat_scalar_window, (("gy", 0), ("gz", 1)), 1)
    northern_adjacent = haloed_array[2:, 1:-1]
    southern_adjacent = haloed_array[:-2, 1:-1]
    ceiling_adjacent = haloed_array[1:-1, 2:]
    bottom_adjacent = haloed_array[1:-1, :-2]
    haloed_array_east = jnp.pad(heat_scalar_window, ((0, 0), (0, 0), (1, 1)))
    eastern_adjacent = haloed_array_east[:, :, 2:]
    western_adjacent = haloed_array_east[:, :, :-2]
    laplacian_contribution = (
        eastern_adjacent
        + western_adjacent
        + northern_adjacent
        + southern_adjacent
        + ceiling_adjacent
        + bottom_adjacent
        - 6.0 * heat_scalar_window
    )
    retained_remainder = (
        flow_speed_vector[0].astype(jnp.float32) * (eastern_adjacent - western_adjacent)
        + flow_speed_vector[1].astype(jnp.float32) * (northern_adjacent - southern_adjacent)
        + flow_speed_vector[2].astype(jnp.float32) * (ceiling_adjacent - bottom_adjacent)
    )
    forcing_contribution = (
        heat_scalar_window
        + thermal_conduction_coefficient * laplacian_contribution
        - 0.5 * retained_remainder
    )
    northward_extent, vertical_extent, eastward_extent = heat_scalar_window.shape
    block_count = eastward_extent // XB
    unit_two = jnp.eye(2, dtype=jnp.float32)
    inverse_x = line_inverse(XB, RX)
    local_x = jnp.dot(
        forcing_contribution.reshape(northward_extent, vertical_extent, block_count, XB),
        inverse_x,
        precision=EXACT,
    )
    ends_x = jnp.stack([local_x[..., 0], local_x[..., -1]])
    lower_x, upper_x = couplers(inverse_x, RX)
    chained = solve_chain(
        jnp.moveaxis(ends_x, 3, 0), reduced_factors(lower_x, upper_x, block_count), lower_x, upper_x
    )
    before_x = jnp.moveaxis(chained[:, 0], 0, 2)
    after_x = jnp.moveaxis(chained[:, 1], 0, 2)
    along_x = (
        local_x
        + RX * inverse_x[:, 0] * before_x[..., None]
        + RX * inverse_x[:, -1] * after_x[..., None]
    )
    along_x = along_x.reshape(northward_extent, vertical_extent, eastward_extent)
    inverse_y = line_inverse(northward_extent, RY)
    local_y = jnp.einsum("ab,bzx->azx", inverse_y, along_x, precision=EXACT)
    ends_y = jnp.stack([local_y[0], local_y[-1]])
    lower_y, upper_y = couplers(inverse_y, RY)
    dinvs_y = reduced_factors(lower_y, upper_y, lax.axis_size("gy"))
    position = lax.axis_index("gy")
    active = (position > 0).astype(jnp.float32)
    factor_here = dinvs_y[position]
    factor_prior = dinvs_y[jnp.maximum(position - 1, 0)]
    carry_map = product_two(lower_y, factor_prior) * active
    blank_pair = jnp.zeros_like(ends_y)
    prior_value = prefix((carry_map, ends_y), "gy", compose, (unit_two, blank_pair), False)[1]
    swept = ends_y + apply_two(carry_map, prior_value)
    step_back = product_two(factor_here, upper_y)
    offset = apply_two(factor_here, swept)
    after_pair = prefix((step_back, offset), "gy", compose, (unit_two, blank_pair), True)[1]
    own_pair = apply_two(step_back, after_pair) + offset
    before_y = apply_two(factor_prior, prior_value + apply_two(upper_y, own_pair))[1] * active
    after_y = after_pair[0]
    along_y = (
        local_y
        + (RY * inverse_y[:, 0])[:, None, None] * before_y[None]
        + (RY * inverse_y[:, -1])[:, None, None] * after_y[None]
    )
    inverse_z = line_inverse(vertical_extent, RZ)
    local_z = jnp.einsum("ab,ybx->yax", inverse_z, along_y, precision=EXACT)
    ends_z = jnp.stack([local_z[:, 0], local_z[:, -1]])
    lower_z, upper_z = couplers(inverse_z, RZ)
    dinvs_z = reduced_factors(lower_z, upper_z, lax.axis_size("gz"))
    position_z = lax.axis_index("gz")
    active_z = (position_z > 0).astype(jnp.float32)
    factor_here_z = dinvs_z[position_z]
    factor_prior_z = dinvs_z[jnp.maximum(position_z - 1, 0)]
    carry_map_z = product_two(lower_z, factor_prior_z) * active_z
    blank_pair_z = jnp.zeros_like(ends_z)
    prior_value_z = prefix((carry_map_z, ends_z), "gz", compose, (unit_two, blank_pair_z), False)[1]
    swept_z = ends_z + apply_two(carry_map_z, prior_value_z)
    step_back_z = product_two(factor_here_z, upper_z)
    offset_z = apply_two(factor_here_z, swept_z)
    after_pair_z = prefix((step_back_z, offset_z), "gz", compose, (unit_two, blank_pair_z), True)[1]
    own_pair_z = apply_two(step_back_z, after_pair_z) + offset_z
    before_z = (
        apply_two(factor_prior_z, prior_value_z + apply_two(upper_z, own_pair_z))[1] * active_z
    )
    after_z = after_pair_z[0]
    updated = (
        local_z
        + (RZ * inverse_z[:, 0])[None, :, None] * before_z[:, None, :]
        + (RZ * inverse_z[:, -1])[None, :, None] * after_z[:, None, :]
    )
    return updated


def solution(mesh):
    in_specs = (P("gy", "gz", None), P(None, "gy", "gz", None))
    out_specs = P("gy", "gz", None)
    return jax.shard_map(
        on_device, mesh=mesh, in_specs=in_specs, out_specs=out_specs, check_vma=False
    )
```

profile of v0, /device:TPU:0, one launch (start us, length us, event | category | flops | bytes accessed | tf_op | source)
XLA Modules:
  0.0 571.0 jit_solution(15180322955402819166)
XLA Ops:
  7.4 4.8 collective-permute-start.1
  17.0 110.5 %while.125 = (s32[]{:T(128)}, f32[2,2]{1,0:T(2,128)S(1)}, f32[15,2,2]{2,1,0:T(2,128)S(1)}, f32[2,2]{1,0:T(2,128)S(1)}, f32[2,2]{1,0:T(2,128)S(1)}, /*index=5*/s32[]{:T(128)}) while((s32[]{:T(128)}, f32[2,2]{1,0:T(2,128)S(1)}, f32[15,2,2]{2,1,0:T(2,128)S(1)}, f32[2,2]{1,0:T(2,128)S(1)}, f32[2,2]{1,0:T(2,128)S(1)}, ...), condition=%wide.region_3.4_spmd.clone, body=%wide.region_0.3_spmd.clone.sunk | while | flops 67 | bytes 2437 | solution.py:110
  132.6 3.0 collective-permute-start.3
  141.7 51.3 %while.123 = (s32[]{:T(128)}, f32[2,16,8]{1,2,0:T(8,128)S(1)}, f32[15,2,16,8]{2,3,1,0:T(8,128)S(1)}, f32[15,2,16,8]{2,3,1,0:T(8,128)S(1)}, f32[2,2]{1,0:T(2,128)S(1)}, /*index=5*/f32[15,2,2]{2,1,0:T(2,128)S(1)}, s32[]{:T(128)}) while((s32[]{:T(128)}, f32[2,16,8]{1,2,0:T(8,128)S(1)}, f32[15,2,16,8]{2,3,1,0:T(8,128)S(1)}, ...), condition=%wide.region_6.7_spmd, body=%wide.region_4.6_spmd.sunk | while | flops 1806 | bytes 29913 | solution.py:122
  142.5 2.6 multiply_add_fusion.40
  145.9 2.6 multiply_add_fusion.40
  149.3 2.6 multiply_add_fusion.40
  152.7 2.6 multiply_add_fusion.40
  156.2 2.6 multiply_add_fusion.40
  159.6 2.6 multiply_add_fusion.40
  163.0 2.6 multiply_add_fusion.40
  166.4 2.6 multiply_add_fusion.40
  169.8 2.6 multiply_add_fusion.40
  195.6 95.2 %while.124 = (s32[]{:T(128)}, f32[2,16,8]{1,2,0:T(8,128)S(1)}, f32[15,2,16,8]{2,3,1,0:T(8,128)S(1)}, f32[15,2,2]{2,1,0:T(2,128)S(1)}, f32[15,2,16,8]{2,3,1,0:T(8...) while((s32[]{:T(128)}, f32[2,16,8]{1,2,0:T(8,128)S(1)}, ...), condition=%wide.region_8.9_spmd, body=%wide.region_7.8_spmd.sunk | while | flops 2307 | bytes 31989 | solution.py:131
  294.4 51.1 %while.126 = (s32[]{:T(128)}, f32[2,2]{1,0:T(2,128)S(1)}, f32[7,2,2]{2,1,0:T(2,128)S(1)}, f32[2,2]{1,0:T(2,128)S(1)}, f32[2,2]{1,0:T(2,128)S(1)}, /*index=5*/s32[]{:T(128)}) while((s32[]{:T(128)}, f32[2,2]{1,0:T(2,128)S(1)}, f32[7,2,2]{2,1,0:T(2,128)S(1)}, f32[2,2]{1,0:T(2,128)S(1)}, f32[2,2]{1,0:T(2,128)S(1)}, ...), condition=%wide.region_12.13_spmd.clone, body=%wide.region_9.12_spmd.clone.sunk | while | flops 67 | bytes 2437 | solution.py:110
  345.9 21.9 %all-gather.8 = f32[8,2,2]{2,1,0:T(2,128)S(1)} all-gather(f32[1,2,2]{2,1,0:T(2,128)S(1)} %fusion.155), channel_id=2, replica_groups=mesh['gy'=8,'gz'=4] {'gy'}, dimensions={0}, use_global_device_ids=true | all-gather | bytes 144 | tf_op jit(solution)/shard_map/all_gather | solution.py:35
  369.1 28.5 %while.128 = (s32[]{:T(128)}, f32[2,8,2048]{2,1,0:T(8,128)S(1)}, s32[]{:T(128)}, f32[8,2,2]{2,1,0:T(2,128)S(1)}, f32[8,2,8,2048]{3,2,1,0:T(8,128)}, /*index=5*/s32[]{:T(128)}, s32[]{:T(128)}) while((s32[]{:T(128)}, f32[2,8,2048]{2,1,0:T(8,128)S(1)}, s32[]{:T(128)}, f32[8,2,2]{2,1,0:T(2,128)S(1)}, f32[8,2,8,2048]{3,2,1,0:T(8,128)}, ...), condition=%wide.region_15.16_spmd.clone, body=%wide.region_14.15_spmd.clone.sunk | while | flops 262148 | bytes 1048762 | solution.py:47
  404.2 16.5 %all-gather.9 = f32[8,2,2]{2,1,0:T(2,128)S(1)} all-gather(f32[1,2,2]{2,1,0:T(2,128)S(1)} %bitcast.395), channel_id=4, replica_groups=mesh['gy'=8,'gz'=4] {'gy'}, dimensions={0}, use_global_device_ids=true | all-gather | bytes 144 | tf_op jit(solution)/shard_map/all_gather | solution.py:35
  425.2 19.6 %all-gather.19.cloned.1.call-done = f32[16,8,2048]{2,1,0:T(8,128)} async-done(((f32[2,8,2048]{2,1,0:T(8,128)}), f32[16,8,2048]{2,1,0:T(8,128)}) %all-gather.19.cloned.1.call-update) | async-done | bytes 1048592 | tf_op jit(solution)/shard_map/all_gather | solution.py:35
  446.1 22.6 %while.129 = (s32[]{:T(128)}, f32[2,8,2048]{2,1,0:T(8,128)S(1)}, s32[]{:T(128)}, f32[8,2,2]{2,1,0:T(2,128)S(1)}, f32[8,2,8,2048]{3,2,1,0:T(8,128)S(1)}, /*index=5*/s32[]{:T(128)}, s32[]{:T(128)}) while((s32[]{:T(128)}, f32[2,8,2048]{2,1,0:T(8,128)S(1)}, s32[]{:T(128)}, f32[8,2,2]{2,1,0:T(2,128)S(1)}, ...), condition=%wide.region_18.19_spmd.clone, body=%wide.region_17.18_spmd.clone.sunk | while | flops 262148 | bytes 1048762 | solution.py:47
  468.8 2.6 multiply_add_fusion.28
  471.7 2.6 multiply_add_fusion.26
  479.2 22.2 %while.127 = (s32[]{:T(128)}, f32[2,2]{1,0:T(2,128)S(1)}, f32[3,2,2]{2,1,0:T(2,128)S(1)}, f32[2,2]{1,0:T(2,128)S(1)}, f32[2,2]{1,0:T(2,128)S(1)}, /*index=5*/s32[]{:T(128)}) while((s32[]{:T(128)}, f32[2,2]{1,0:T(2,128)S(1)}, f32[3,2,2]{2,1,0:T(2,128)S(1)}, f32[2,2]{1,0:T(2,128)S(1)}, f32[2,2]{1,0:T(2,128)S(1)}, ...), condition=%wide.region_22.23_spmd.clone, body=%wide.region_19.22_spmd.clone.sunk | while | flops 67 | bytes 2437 | solution.py:110
  501.6 5.1 all-gather.10
  508.0 12.9 %while.130 = (s32[]{:T(128)}, f32[2,16,2048]{2,1,0:T(8,128)S(1)}, s32[]{:T(128)}, f32[4,2,2]{2,1,0:T(2,128)S(1)}, f32[4,2,16,2048]{3,2,1,0:T(8,128)}, /*index=5*/s32[]{:T(128)}, s32[]{:T(128)}) while((s32[]{:T(128)}, f32[2,16,2048]{2,1,0:T(8,128)S(1)}, s32[]{:T(128)}, f32[4,2,2]{2,1,0:T(2,128)S(1)}, ...), condition=%wide.region_25.26_spmd.clone, body=%wide.region_24.25_spmd.clone.sunk | while | flops 524292 | bytes 2097338 | solution.py:47
  521.1 2.7 multiply_add_fusion.24
  524.3 2.8 multiply_add_fusion.22
  528.3 5.1 all-gather.11
  535.9 8.0 %all-gather.23.cloned.1.call-done = f32[8,16,2048]{2,1,0:T(8,128)} async-done(((f32[2,16,2048]{2,1,0:T(8,128)}), f32[8,16,2048]{2,1,0:T(8,128)}) %all-gather.23.cloned.1.call-update) | async-done | bytes 1048592 | tf_op jit(solution)/shard_map/all_gather | solution.py:35
  545.2 9.9 %while.131 = (s32[]{:T(128)}, f32[2,16,2048]{2,1,0:T(8,128)S(1)}, s32[]{:T(128)}, f32[4,2,2]{2,1,0:T(2,128)S(1)}, f32[4,2,16,2048]{3,2,1,0:T(8,128)S(1)}, /*index=5*/s32[]{:T(128)}, s32[]{:T(128)}) while((s32[]{:T(128)}, f32[2,16,2048]{2,1,0:T(8,128)S(1)}, s32[]{:T(128)}, f32[4,2,2]{2,1,0:T(2,128)S(1)}, ...), condition=%wide.region_28.29_spmd.clone, body=%wide.region_27.28_spmd.clone.sunk | while | flops 524292 | bytes 2097338 | solution.py:47
  555.3 2.8 multiply_add_fusion.20
  558.6 2.7 multiply_add_fusion.18
  (631 shorter events, 333.2 us)
Async XLA Ops:
  6.5 362.6 %all-gather.17.cloned.1.call-start = ((), (), s32[]{:S(2)}) async-start(), calls=%async_computation | async-start | bytes 1179648 | tf_op jit(solution)/shard_map/all_gather | solution.py:35
  7.4 122.3 %collective-permute-start.1 = (f32[1,8,2048]{2,1,0:T(8,128)S(1)}, f32[1,8,2048]{2,1,0:T(8,128)S(1)}, u32[]{:S(2)}, u32[]{:S(2)}) collective-permute-start(f32[1,8,2048]{2,1,0:T(8,128)S(1)} %get-tuple-element.1031), channel_id=1, source_target_pairs={{0,4},{4,8},{8,12},{12,16},{16,20},{20,24},{24,28},{1,5},{5,9},{9,... | collective-permute-start | bytes 196616 | tf_op jit(solution)/shard_map/ppermute | solution.py:24
  12.3 118.8 %collective-permute-start = (f32[1,8,2048]{2,1,0:T(8,128)S(1)}, f32[1,8,2048]{2,1,0:T(8,128)S(1)}, u32[]{:S(2)}, u32[]{:S(2)}) collective-permute-start(f32[1,8,2048]{2,1,0:T(8,128)S(1)} %get-tuple-element.1030), channel_id=1, source_target_pairs={{4,0},{8,4},{12,8},{16,12},{20,16},{24,20},{28,24},{5,1},{9,5},{13... | collective-permute-start | bytes 196616 | tf_op jit(solution)/shard_map/ppermute | solution.py:26
  16.9 118.8 %copy-start.1 = (f32[2,2]{1,0:T(2,128)}, f32[2,2]{1,0:T(2,128)S(1)}, u32[]{:S(2)}) copy-start(f32[2,2]{1,0:T(2,128)S(1)} %compare_convert_fusion.4) | copy-start | bytes 52
  129.7 6.9 %copy-start = (f32[16,8,2048]{2,1,0:T(8,128)S(1)}, f32[16,8,2048]{2,1,0:T(8,128)}, u32[]{:S(2)}) copy-start(f32[16,8,2048]{2,1,0:T(8,128)} %param.20) | copy-start | bytes 3145732
  131.3 5.1 collective-permute-start.2
  132.6 4.0 collective-permute-start.3
  291.9 2.6 copy-start.3
  294.4 150.4 %all-gather.19.cloned.1.call-start = ((), (), s32[]{:S(2)}) async-start(), calls=%async_computation.1 | async-start | bytes 1179648 | tf_op jit(solution)/shard_map/all_gather | solution.py:35
  404.1 103.9 %all-gather.21.cloned.1.call-start = ((), (), s32[]{:S(2)}) async-start(), calls=%async_computation.2 | async-start | bytes 1310720 | tf_op jit(solution)/shard_map/all_gather | solution.py:35
  477.8 1.4 copy-start.2
  479.1 64.8 %all-gather.23.cloned.1.call-start = ((), (), s32[]{:S(2)}) async-start(), calls=%async_computation.3 | async-start | bytes 1310720 | tf_op jit(solution)/shard_map/all_gather | solution.py:35
Sparse Core Ops, SparseCore 0:
  294.5 45.6 all-gather.16
  404.2 40.5 all-gather.18
  479.3 15.4 all-gather.20
  528.4 15.4 all-gather.22
where the time goes:
time: 577 us; the launch traced here: 571 us
  other arithmetic  286 us (50%)
  loops' own time  97.7 us (17%)
  local copies, waits for them, and re-layouts  80.2 us (14%)
  blocking collectives  48.5 us (8%)
  waiting for transfers between devices  27.8 us (5%)
  between operations  16.4 us (3%)
  starting transfers between devices  10.6 us (2%)
    add x74, other arithmetic, apply_two(): matrix[0, 0] * vector[0] + matrix[0, 1] * vector[1]  187 us
    another operation x3, loops' own time, reduced_factors(): lax.scan(advance, unit_two, None, length=line_count - 1)  95.3 us
    another operation x50, other arithmetic, inverse_two(): jnp.stack([jnp.stack([matrix[1, 1], -matrix[0, 1]]), jnp.stack([-matrix[1...  66.6 us
    all_gather x4, blocking collectives, prefix(): pieces = jax.tree.map(lambda part: lax.all_gather(part, axis), value)  48.5 us
    slice x74, local copies, waits for them, and re-layouts, apply_two(): matrix[0, 0] * vector[0] + matrix[0, 1] * vector[1]  47.8 us
    all_gather x4, waiting for transfers between devices, prefix(): pieces = jax.tree.map(lambda part: lax.all_gather(part, axis), value)  27.6 us
    slice x25, local copies, waits for them, and re-layouts, inverse_two(): matrix[1, 1]  16.4 us
  transfers between devices with their start and end apart: 8, of which 3 were waited for; matrix products, arithmetic and copies ran while one was open for 18% of the time, Pallas kernels for 0%

commit v1 on v0

v1 whole, which is shorter than its diff:
```python
import functools

import jax
import jax.numpy as jnp
import numpy as np
from jax import lax
from jax.experimental import pallas as pl
from jax.experimental.pallas import tpu as pltpu
from jax.sharding import PartitionSpec as P

RX = 1
RY = 768
RZ = 192
KAPPA = 0.15
XB = 256
LANES = 128
MESH = pl.DeviceIdType.MESH


def decay(ratio):
    h = 0.5 / ratio
    return 1.0 + h - np.sqrt(h * (2.0 + h))


def line_parts(n, ratio):
    q = decay(ratio)
    i = np.arange(n, dtype=np.float64)
    half = n / 2.0
    rise = q ** (-i + half) * (1.0 - q ** (2.0 * (i + 1.0)))
    fall = q ** (i + 1.0 - half) * (1.0 - q ** (2.0 * (n - i)))
    fall = fall / (ratio * (1.0 - q * q) * (1.0 - q ** (2.0 * n + 2.0)))
    return rise, fall


def line_block(rise, fall):
    n = len(rise)
    small = np.minimum(np.arange(n)[:, None], np.arange(n)[None, :])
    large = np.maximum(np.arange(n)[:, None], np.arange(n)[None, :])
    return rise[small] * fall[large]


def sizes(ny, nz, ly, lz):
    rows = ly * lz
    far_y = rows
    far_z = far_y + 2 * lz
    corner = far_z + nz * ly
    total = corner + -(-2 * nz // 8) * 8
    return rows, far_y, far_z, corner, total


def tables(ny, nz, ly, lz):
    rows, far_y, far_z, corner, total = sizes(ny, nz, ly, lz)
    ry, fy = line_parts(ny * ly, RY)
    rz, fz = line_parts(nz * lz, RZ)
    ry, fy = ry.reshape(ny, ly), fy.reshape(ny, ly)
    rz, fz = rz.reshape(nz, lz), fz.reshape(nz, lz)
    ey = np.zeros((ny, ly, lz, total))
    ez = np.zeros((nz, ly, lz, total))
    for a in range(ny):
        block = line_block(ry[a], fy[a])
        ey[a, :, :, :rows] = np.repeat(block, lz, axis=1)[:, None, :]
        ey[a, :, :, far_y : far_y + lz] = fy[a][:, None, None]
        ey[a, :, :, far_y + lz : far_z] = ry[a][:, None, None]
        ey[a, :, :, far_z:corner] = np.tile(block, (1, nz))[:, None, :]
        ey[a, :, :, corner : corner + 2 * nz : 2] = fy[a][:, None, None]
        ey[a, :, :, corner + 1 : corner + 2 * nz : 2] = ry[a][:, None, None]
    for c in range(nz):
        block = line_block(rz[c], fz[c])
        ez[c, :, :, :far_z] = np.tile(block, (1, ly + 2))[None]
        for b in range(nz):
            weight = fz[c] if b < c else rz[c]
            if b != c:
                ez[c, :, :, far_z + b * ly : far_z + (b + 1) * ly] = weight[None, :, None]
                ez[c, :, :, corner + 2 * b : corner + 2 * b + 2] = weight[None, :, None]
    coef = np.concatenate([ry.reshape(-1), fy.reshape(-1)])
    zw = np.stack([rz, fz], axis=1)[..., None] * np.ones(LANES)
    f32 = lambda t: np.asarray(t, np.float32)
    return (
        f32(coef),
        f32(zw),
        f32(ey.reshape(ny, rows, total)),
        f32(ez.reshape(nz, rows, total)),
    )


def x_tables():
    q = decay(RX)
    i = np.arange(XB)
    toep = q ** np.abs(i[:, None] - i[None, :]) * q / (RX * (1.0 - q * q))
    toep = np.asarray(toep, np.float32)
    hi = toep.astype(jnp.bfloat16)
    lo = (toep - hi.astype(np.float32)).astype(jnp.bfloat16)
    uw = np.stack([q ** (i + 1.0), q ** (XB - i * 1.0)])[:, None, :] * np.ones((1, 8, 1))
    return np.stack([hi, lo]), np.asarray(uw, np.float32)


def split(x):
    hi = x.astype(jnp.bfloat16)
    return hi, (x - hi.astype(jnp.float32)).astype(jnp.bfloat16)


def dot(a, b):
    return jnp.dot(a, b, preferred_element_type=jnp.float32)


def dot3(a, b):
    return dot(a[0], b[0]) + (dot(a[1], b[0]) + dot(a[0], b[1]))


def kernel(
    ny, nz, owners,
    heat, speed, coef, zw, ey_hbm, ez_hbm, toep, uw,
    out,
    field, vel, zsend, zhalo, data, yface, zface, held, back, cface, chold, ey, ez,
    load_sem, hs_send, hs_recv, a_send, a_recv, b_send, b_recv, z_send, z_recv, c_send, c_recv,
):
    ly, lz, nx = heat.shape
    rows, far_y, far_z, corner, total = sizes(ny, nz, ly, lz)
    cw = nx // owners
    my = lax.axis_index("gy")
    mz = lax.axis_index("gz")

    loads = [
        pltpu.make_async_copy(heat, field.at[pl.ds(1, ly)], load_sem.at[0]),
        pltpu.make_async_copy(speed, vel, load_sem.at[1]),
        pltpu.make_async_copy(ey_hbm.at[my], ey, load_sem.at[2]),
        pltpu.make_async_copy(ez_hbm.at[mz], ez, load_sem.at[3]),
    ]
    for load in loads:
        load.start()

    barrier = pltpu.get_barrier_semaphore()
    for d in range(1, ny):
        pl.semaphore_signal(barrier, 1, device_id={"gy": lax.rem(my + d, ny)}, device_id_type=MESH)
    for d in range(1, nz):
        pl.semaphore_signal(barrier, 1, device_id={"gz": lax.rem(mz + d, nz)}, device_id_type=MESH)

    loads[0].wait()
    for y in range(ly):
        zsend[0, y : y + 1, :] = field[y + 1, 0:1, :]
        zsend[1, y : y + 1, :] = field[y + 1, lz - 1 : lz, :]
    pl.semaphore_wait(barrier, ny - 1 + nz - 1)

    def remote(src, dst, send, recv, target):
        return pltpu.make_async_remote_copy(
            src_ref=src, dst_ref=dst, send_sem=send, recv_sem=recv,
            device_id=target, device_id_type=MESH,
        )

    down_y = lax.rem(my + ny - 1, ny)
    up_y = lax.rem(my + 1, ny)
    down_z = lax.rem(mz + nz - 1, nz)
    up_z = lax.rem(mz + 1, nz)
    y_down = remote(field.at[1], field.at[ly + 1], hs_send.at[0], hs_recv.at[0], {"gy": down_y})
    y_up = remote(field.at[ly], field.at[0], hs_send.at[1], hs_recv.at[1], {"gy": up_y})
    z_down = remote(zsend.at[0], zhalo.at[1], hs_send.at[2], hs_recv.at[2], {"gz": down_z})
    z_up = remote(zsend.at[1], zhalo.at[0], hs_send.at[3], hs_recv.at[3], {"gz": up_z})
    first_y, last_y = my == 0, my == ny - 1
    first_z, last_z = mz == 0, mz == nz - 1

    @pl.when(jnp.logical_not(last_z))
    def _():
        z_up.start()

    @pl.when(jnp.logical_not(first_z))
    def _():
        z_down.start()

    @pl.when(jnp.logical_not(last_y))
    def _():
        y_up.start()

    @pl.when(jnp.logical_not(first_y))
    def _():
        y_down.start()

    @pl.when(first_y)
    def _():
        field[0] = jnp.zeros((lz, nx), jnp.float32)

    @pl.when(last_y)
    def _():
        field[ly + 1] = jnp.zeros((lz, nx), jnp.float32)

    @pl.when(first_z)
    def _():
        zhalo[0] = jnp.zeros((ly, nx), jnp.float32)

    @pl.when(last_z)
    def _():
        zhalo[1] = jnp.zeros((ly, nx), jnp.float32)

    data[pl.ds(pl.multiple_of(far_z + mz * ly, 8), ly), :] = jnp.zeros((ly, nx), jnp.float32)
    data[corner:total, :] = jnp.zeros((total - corner, nx), jnp.float32)
    for load in loads[1:]:
        load.wait()
    weights = split(ey[...] * ez[...])

    @pl.when(jnp.logical_not(first_y))
    def _():
        y_up.wait_recv()

    @pl.when(jnp.logical_not(last_y))
    def _():
        y_down.wait_recv()

    @pl.when(jnp.logical_not(first_z))
    def _():
        z_up.wait_recv()

    @pl.when(jnp.logical_not(last_z))
    def _():
        z_down.wait_recv()

    tile = lambda w: jnp.concatenate([w] * (nx // LANES), axis=1)
    rise_z = tile(zw[mz, 0])
    fall_z = tile(zw[mz, 1])
    level = lax.broadcasted_iota(jnp.int32, (lz, nx), 0)
    place = lax.broadcasted_iota(jnp.int32, (lz, nx), 1)
    yface[...] = jnp.zeros_like(yface)

    def layer(y, _):
        here = field[y + 1]
        south, north = field[y], field[y + 2]
        above = jnp.where(level == lz - 1, zhalo[1, pl.ds(y, 1), :], pltpu.roll(here, lz - 1, 0))
        below = jnp.where(level == 0, zhalo[0, pl.ds(y, 1), :], pltpu.roll(here, 1, 0))
        east = jnp.where(place == nx - 1, 0.0, pltpu.roll(here, nx - 1, 1))
        west = jnp.where(place == 0, 0.0, pltpu.roll(here, 1, 1))
        spread = east + west + north + south + above + below - 6.0 * here
        moved = (
            vel[0, y].astype(jnp.float32) * (east - west)
            + vel[1, y].astype(jnp.float32) * (north - south)
            + vel[2, y].astype(jnp.float32) * (above - below)
        )
        source = here + KAPPA * spread - 0.5 * moved
        data[pl.ds(pl.multiple_of(y * lz, lz), lz), :] = source
        yface[0:lz, :] += coef[my * ly + y] * source
        yface[lz : 2 * lz, :] += coef[ny * ly + my * ly + y] * source
        zface[0, pl.ds(y, 1), :] = jnp.sum(source * rise_z, axis=0, keepdims=True)
        zface[1, pl.ds(y, 1), :] = jnp.sum(source * fall_z, axis=0, keepdims=True)
        return 0

    lax.fori_loop(0, ly, layer, 0)

    def to_owner(owner):
        return remote(
            yface.at[:, pl.ds(pl.multiple_of(owner * cw, LANES), cw)], held.at[my],
            a_send.at[owner], a_recv.at[my], {"gy": owner},
        )

    def from_peer(peer):
        return remote(
            yface.at[:, pl.ds(0, cw)], held.at[peer], a_send.at[0], a_recv.at[peer], {"gy": peer}
        )

    def owned(index, body):
        if owners == ny:
            body()
        else:
            pl.when(index < owners)(body)

    for d in range(1, ny):
        peer = lax.rem(my + d, ny)
        owned(peer, lambda peer=peer: to_owner(peer).start())

    z_copies = []
    for d in range(1, nz):
        peer = lax.rem(mz + d, nz)
        side = (mz + d) // nz
        slot = data.at[pl.ds(pl.multiple_of(far_z + mz * ly, 8), ly)]
        copy = remote(zface.at[side], slot, z_send.at[peer], z_recv.at[mz], {"gz": peer})
        copy.start()
        z_copies.append(copy)

    def to_peer(peer):
        return remote(
            back.at[peer],
            data.at[pl.ds(far_y, 2 * lz), pl.ds(pl.multiple_of(my * cw, LANES), cw)],
            b_send.at[peer], b_recv.at[my], {"gy": peer},
        )

    def from_owner(owner):
        return remote(
            back.at[0],
            data.at[pl.ds(far_y, 2 * lz), pl.ds(pl.multiple_of(owner * cw, LANES), cw)],
            b_send.at[0], b_recv.at[owner], {"gy": owner},
        )

    def gather_sums():
        held[my] = yface[:, pl.ds(pl.multiple_of(my * cw, LANES), cw)]
        for d in range(1, ny):
            from_peer(lax.rem(my + d, ny)).wait_recv()
        run = jnp.zeros((lz, cw), jnp.float32)
        for a in range(ny):
            back[a, 0:lz, :] = run
            run = run + held[a, 0:lz, :]
        run = jnp.zeros((lz, cw), jnp.float32)
        for a in reversed(range(ny)):
            back[a, lz : 2 * lz, :] = run
            run = run + held[a, lz : 2 * lz, :]
        for d in range(1, ny):
            to_peer(lax.rem(my + d, ny)).start()
        data[far_y : far_y + 2 * lz, pl.ds(pl.multiple_of(my * cw, LANES), cw)] = back[my]

    owned(my, gather_sums)
    for d in range(1, ny):
        owner = lax.rem(my + d, ny)
        owned(owner, lambda owner=owner: from_owner(owner).wait_recv())

    for k in range(2):
        far = data[far_y + k * lz : far_y + (k + 1) * lz, :]
        cface[0, :, k * nx : (k + 1) * nx] = jnp.sum(far * rise_z, axis=0, keepdims=True)
        cface[1, :, k * nx : (k + 1) * nx] = jnp.sum(far * fall_z, axis=0, keepdims=True)
    c_copies = []
    for d in range(1, nz):
        peer = lax.rem(mz + d, nz)
        side = (mz + d) // nz
        copy = remote(cface.at[side], chold.at[mz], c_send.at[peer], c_recv.at[mz], {"gz": peer})
        copy.start()
        c_copies.append(copy)
    chold[mz] = jnp.zeros((1, 2 * nx), jnp.float32)
    for d in range(1, nz):
        peer = lax.rem(mz + d, nz)
        slot = data.at[pl.ds(pl.multiple_of(far_z + peer * ly, 8), ly)]
        remote(zface.at[0], slot, z_send.at[0], z_recv.at[peer], {"gz": peer}).wait_recv()
        remote(
            cface.at[0], chold.at[peer], c_send.at[0], c_recv.at[peer], {"gz": peer}
        ).wait_recv()
    for b in range(nz):
        for k in range(2):
            data[corner + 2 * b + k : corner + 2 * b + k + 1, :] = chold[b, :, k * nx : (k + 1) * nx]

    blocks = nx // XB
    toeplitz = (toep[0], toep[1])
    heads, tails = [], []
    for a in range(blocks):
        part = slice(a * XB, (a + 1) * XB)
        mixed = dot3(weights, split(data[:, part]))
        local = dot3(split(mixed), toeplitz)
        out[:, part] = local
        heads.append(local[:, 0:1])
        tails.append(local[:, XB - 1 : XB])
    q = decay(RX)
    step = float(q**XB)
    head, tail = heads[-1], tails[0]
    for a in range(1, blocks):
        tail = step * tail + tails[a]
        head = step * head + heads[blocks - 1 - a]
    scale = 1.0 / (1.0 - q ** (2.0 * nx + 2.0))
    near, far = float(-q * scale), float(q ** (nx + 2.0) * scale)
    ahead = [near * head + far * tail]
    after = [near * tail + far * head]
    for a in range(blocks - 1):
        ahead.append(step * ahead[-1] + tails[a])
        after.append(step * after[-1] + heads[blocks - 1 - a])
    after = after[::-1]
    grow, fade = uw[0, 0:1, :], uw[1, 0:1, :]
    for a in range(blocks):
        part = slice(a * XB, (a + 1) * XB)
        out[:, part] += ahead[a] * grow + after[a] * fade

    @pl.when(jnp.logical_not(last_z))
    def _():
        z_up.wait_send()

    @pl.when(jnp.logical_not(first_z))
    def _():
        z_down.wait_send()

    @pl.when(jnp.logical_not(last_y))
    def _():
        y_up.wait_send()

    @pl.when(jnp.logical_not(first_y))
    def _():
        y_down.wait_send()

    for d in range(1, ny):
        peer = lax.rem(my + d, ny)
        owned(peer, lambda peer=peer: to_owner(peer).wait_send())
    for copy in z_copies + c_copies:
        copy.wait_send()

    def sums_sent():
        for d in range(1, ny):
            to_peer(lax.rem(my + d, ny)).wait_send()

    owned(my, sums_sent)


def on_device(ny, nz, heat, speed):
    ly, lz, nx = heat.shape
    rows, far_y, far_z, corner, total = sizes(ny, nz, ly, lz)
    owners = min(ny, nx // LANES)
    while (nx // LANES) % owners:
        owners -= 1
    cw = nx // owners
    coef, zw, ey, ez = tables(ny, nz, ly, lz)
    toep, uw = x_tables()
    hbm = pl.BlockSpec(memory_space=pl.ANY)
    vmem = pl.BlockSpec(memory_space=pltpu.VMEM)
    smem = pl.BlockSpec(memory_space=pltpu.SMEM)
    dma = pltpu.SemaphoreType.DMA
    f32 = jnp.float32
    out = pl.pallas_call(
        functools.partial(kernel, ny, nz, owners),
        out_shape=jax.ShapeDtypeStruct((rows, nx), f32),
        in_specs=[hbm, hbm, smem, vmem, hbm, hbm, vmem, vmem],
        out_specs=vmem,
        scratch_shapes=[
            pltpu.VMEM((ly + 2, lz, nx), f32),
            pltpu.VMEM(speed.shape, speed.dtype),
            pltpu.VMEM((2, ly, nx), f32),
            pltpu.VMEM((2, ly, nx), f32),
            pltpu.VMEM((total, nx), f32),
            pltpu.VMEM((2 * lz, nx), f32),
            pltpu.VMEM((2, ly, nx), f32),
            pltpu.VMEM((ny, 2 * lz, cw), f32),
            pltpu.VMEM((ny, 2 * lz, cw), f32),
            pltpu.VMEM((2, 1, 2 * nx), f32),
            pltpu.VMEM((nz, 1, 2 * nx), f32),
            pltpu.VMEM((rows, total), f32),
            pltpu.VMEM((rows, total), f32),
            dma((4,)), dma((4,)), dma((4,)),
            dma((ny,)), dma((ny,)), dma((ny,)), dma((ny,)),
            dma((nz,)), dma((nz,)), dma((nz,)), dma((nz,)),
        ],
        compiler_params=pltpu.CompilerParams(
            collective_id=0, has_side_effects=True, vmem_limit_bytes=40 * 1024 * 1024
        ),
    )(heat, speed, jnp.asarray(coef), jnp.asarray(zw), jnp.asarray(ey), jnp.asarray(ez),
      jnp.asarray(toep), jnp.asarray(uw))
    return out.reshape(ly, lz, nx)


def solution(mesh):
    in_specs = (P("gy", "gz", None), P(None, "gy", "gz", None))
    return jax.shard_map(
        functools.partial(on_device, mesh.shape["gy"], mesh.shape["gz"]),
        mesh=mesh, in_specs=in_specs, out_specs=P("gy", "gz", None), check_vma=False,
    )
```

time: 577 us -> 37.7 us (0.07)
  other arithmetic: 286 us -> 0 us
  loops' own time: 97.7 us -> 0 us
  local copies, waits for them, and re-layouts: 80.2 us -> 8.97 us
  blocking collectives: 48.5 us -> 0 us
  Pallas kernels: 0 us -> 28.3 us
  waiting for transfers between devices: 27.8 us -> 0 us
  between operations: 16.4 us -> 0.02 us
  starting transfers between devices: 10.6 us -> 0 us
    add x113 -> x0, other arithmetic: 191 us -> none  [the longest x74 187 us: apply_two(): matrix[0, 0] * vector[0] + matrix[0, 1] * vector[1]]
    another operation x9 -> x0, loops' own time: 97.7 us -> none  [the longest x3 95.3 us: reduced_factors(): lax.scan(advance, unit_two, None, length=line_count - 1)]
    slice x112 -> x0, local copies, waits for them, and re-layouts: 70.6 us -> none  [the longest x74 47.8 us: apply_two(): matrix[0, 0] * vector[0] + matrix[0, 1] * vector[1]]
    another operation x69 -> x0, other arithmetic: 70.4 us -> none  [the longest x50 66.6 us: inverse_two(): jnp.stack([jnp.stack([matrix[1, 1], -matrix[0, 1]]), jnp.stack([-matrix[1...]
    all_gather x4 -> x0, blocking collectives: 48.5 us -> none  [prefix(): pieces = jax.tree.map(lambda part: lax.all_gather(part, axis), value)]
    pallas_call x0 -> x1, Pallas kernels: none -> 28.3 us  [on_device(): pl.pallas_call(functools.partial(kernel, ny, nz, owners), out_shape=jax.S...]
    all_gather x4 -> x0, waiting for transfers between devices: 27.6 us -> none  [prefix(): pieces = jax.tree.map(lambda part: lax.all_gather(part, axis), value)]
    ppermute x4 -> x0, starting transfers between devices: 10.5 us -> none  [the longest x2 7.88 us: extended(): lax.ppermute(tail, axis, [(i, (i + 1) % count) for i in range(ends)])]
  transfers between devices with their start and end apart: 8 -> 0, of which waited for: 3 -> 0; matrix products, arithmetic and copies ran while one was open for 18% -> 0% of each run, Pallas kernels for 0% -> 0%
where the time goes in v1:
time: 37.7 us; the launch traced here: 37.3 us
  Pallas kernels  28.3 us (75%)
  local copies, waits for them, and re-layouts  8.97 us (24%)
    pallas_call x1, Pallas kernels, on_device(): pl.pallas_call(functools.partial(kernel, ny, nz, owners), out_shape=jax.S...  28.3 us
    unnamed x17, local copies, waits for them, and re-layouts  8.97 us

profile of v1, /device:TPU:0, one launch (start us, length us, event | category | flops | bytes accessed | tf_op | source)
XLA Modules:
  0.0 37.3 jit_solution(16368696698102435776)
XLA Ops:
  0.0 0.0 copy-start
  0.0 1.4 %copy-done = bf16[3,16,8,2048]{3,2,1,0:T(8,128)(2,1)S(1)} copy-done((bf16[3,16,8,2048]{3,2,1,0:T(8,128)(2,1)S(1)}, bf16[3,16,8,2048]{3,2,1,0:T(8,128)(2,1)}, u32[]{:S(2)}) %copy-start) | copy-done | bytes 1572888
  1.4 0.0 copy-start.1
  1.4 1.2 %copy-done.1 = f32[16,8,2048]{2,1,0:T(8,128)S(1)} copy-done((f32[16,8,2048]{2,1,0:T(8,128)S(1)}, f32[16,8,2048]{2,1,0:T(8,128)}, u32[]{:S(2)}) %copy-start.1) | copy-done | bytes 1048600
  2.6 0.0 copy-start.2
  2.6 1.2 %copy-done.2 = f32[8,128,216]{2,1,0:T(8,128)S(1)} copy-done((f32[8,128,216]{2,1,0:T(8,128)S(1)}, f32[8,128,216]{2,1,0:T(8,128)}, u32[]{:S(2)}) %copy-start.2) | copy-done | bytes 884760
  3.9 0.0 copy-start.3
  3.9 1.0 %copy-done.3 = f32[4,128,216]{2,1,0:T(8,128)S(1)} copy-done((f32[4,128,216]{2,1,0:T(8,128)S(1)}, f32[4,128,216]{2,1,0:T(8,128)}, u32[]{:S(2)}) %copy-start.3) | copy-done | bytes 442392
  4.9 0.0 copy-start.4
  4.9 0.9 %copy-done.4 = bf16[2,256,256]{2,1,0:T(8,128)(2,1)S(1)} copy-done((bf16[2,256,256]{2,1,0:T(8,128)(2,1)S(1)}, bf16[2,256,256]{2,1,0:T(8,128)(2,1)}, u32[]{:S(2)}) %copy-start.4) | copy-done | bytes 262168
  5.9 0.0 copy-start.5
  5.9 0.8 %copy-done.5 = f32[4,2,8,128]{3,2,1,0:T(8,128)S(1)} copy-done((f32[4,2,8,128]{3,2,1,0:T(8,128)S(1)}, f32[4,2,8,128]{3,2,1,0:T(8,128)}, u32[]{:S(2)}) %copy-start.5) | copy-done | bytes 32792
  6.6 0.0 copy-start.6
  6.6 0.7 %copy-done.6 = f32[2,8,256]{2,1,0:T(8,128)S(1)} copy-done((f32[2,8,256]{2,1,0:T(8,128)S(1)}, f32[2,8,256]{2,1,0:T(8,128)}, u32[]{:S(2)}) %copy-start.6) | copy-done | bytes 16408
  7.3 0.0 copy-start.7
  7.3 0.7 %copy-done.7 = f32[256]{0:T(256)S(1)} copy-done((f32[256]{0:T(256)S(1)}, f32[256]{0:T(256)}, u32[]{:S(2)}) %copy-start.7) | copy-done | bytes 1048
  8.0 28.3 %shard_map.82 = f32[128,2048]{1,0:T(8,128)S(1)} custom-call(f32[16,8,2048]{2,1,0:T(8,128)S(1)} %copy-done.1, bf16[3,16,8,2048]{3,2,1,0:T(8,128)(2,1)S(1)} %copy-done, f32[256]{0:T(256)S(1)} %copy-done.7, f32[4,2,8,128]{3,2,1,0:T(8,128)S(1)} %copy-done.5, f32[8,128,216]{2,1,0:T(8,128)S(1)} %copy-done.2, f32[4,128,216]{2,1,0:T(8,128)S(1)} %copy-done.3, ...), custom_call_target="tpu_custom_call" | custom-call | tf_op jit(solution)/shard_map/pallas_call | solution.py:405
  36.3 1.0 %copy.10 = f32[16,8,2048]{2,1,0:T(8,128)} copy(f32[16,8,2048]{2,1,0:T(8,128)S(1)} %bitcast.1) | data formatting | bytes 2097152
Async XLA Ops:
  0.0 1.4 %copy-start = (bf16[3,16,8,2048]{3,2,1,0:T(8,128)(2,1)S(1)}, bf16[3,16,8,2048]{3,2,1,0:T(8,128)(2,1)}, u32[]{:S(2)}) copy-start(bf16[3,16,8,2048]{3,2,1,0:T(8,128)(2,1)} %speed.1) | copy-start | bytes 4718596
  1.4 1.2 %copy-start.1 = (f32[16,8,2048]{2,1,0:T(8,128)S(1)}, f32[16,8,2048]{2,1,0:T(8,128)}, u32[]{:S(2)}) copy-start(f32[16,8,2048]{2,1,0:T(8,128)} %heat.1) | copy-start | bytes 3145732
  2.6 1.2 %copy-start.2 = (f32[8,128,216]{2,1,0:T(8,128)S(1)}, f32[8,128,216]{2,1,0:T(8,128)}, u32[]{:S(2)}) copy-start(f32[8,128,216]{2,1,0:T(8,128)} %constant.14.clone.ey_hbm) | copy-start | bytes 2654212
  3.9 1.0 %copy-start.3 = (f32[4,128,216]{2,1,0:T(8,128)S(1)}, f32[4,128,216]{2,1,0:T(8,128)}, u32[]{:S(2)}) copy-start(f32[4,128,216]{2,1,0:T(8,128)} %constant.15.clone.ez_hbm) | copy-start | bytes 1327108
  4.9 0.9 %copy-start.4 = (bf16[2,256,256]{2,1,0:T(8,128)(2,1)S(1)}, bf16[2,256,256]{2,1,0:T(8,128)(2,1)}, u32[]{:S(2)}) copy-start(bf16[2,256,256]{2,1,0:T(8,128)(2,1)} %constant.16.clone.toep) | copy-start | bytes 786436
  5.9 0.8 %copy-start.5 = (f32[4,2,8,128]{3,2,1,0:T(8,128)S(1)}, f32[4,2,8,128]{3,2,1,0:T(8,128)}, u32[]{:S(2)}) copy-start(f32[4,2,8,128]{3,2,1,0:T(8,128)} %constant.13.clone.zw) | copy-start | bytes 98308
  6.6 0.7 %copy-start.6 = (f32[2,8,256]{2,1,0:T(8,128)S(1)}, f32[2,8,256]{2,1,0:T(8,128)}, u32[]{:S(2)}) copy-start(f32[2,8,256]{2,1,0:T(8,128)} %constant.17.clone.uw) | copy-start | bytes 49156
  7.3 0.7 %copy-start.7 = (f32[256]{0:T(256)S(1)}, f32[256]{0:T(256)}, u32[]{:S(2)}) copy-start(f32[256]{0:T(256)} %constant.12.clone.coef) | copy-start | bytes 3076

commit v2 on v1

v2 whole, which is shorter than its diff:
```python
import functools

import jax
import jax.numpy as jnp
import numpy as np
from jax import lax
from jax.experimental import pallas as pl
from jax.experimental.pallas import tpu as pltpu
from jax.sharding import PartitionSpec as P

RX = 1
RY = 768
RZ = 192
KAPPA = 0.15
XB = 256
LANES = 128
MESH = pl.DeviceIdType.MESH


def decay(ratio):
    h = 0.5 / ratio
    return 1.0 + h - np.sqrt(h * (2.0 + h))


def line_parts(n, ratio):
    q = decay(ratio)
    i = np.arange(n, dtype=np.float64)
    half = n / 2.0
    rise = q ** (-i + half) * (1.0 - q ** (2.0 * (i + 1.0)))
    fall = q ** (i + 1.0 - half) * (1.0 - q ** (2.0 * (n - i)))
    fall = fall / (ratio * (1.0 - q * q) * (1.0 - q ** (2.0 * n + 2.0)))
    return rise, fall


def line_block(rise, fall):
    n = len(rise)
    small = np.minimum(np.arange(n)[:, None], np.arange(n)[None, :])
    large = np.maximum(np.arange(n)[:, None], np.arange(n)[None, :])
    return rise[small] * fall[large]


def sizes(ny, nz, ly, lz):
    rows = ly * lz
    far_y = rows + nz * ly
    corner = far_y + 2 * lz
    total = corner + -(-2 * nz // 16) * 16
    return rows, far_y, corner, total


def tables(ny, nz, ly, lz):
    rows, far_y, corner, total = sizes(ny, nz, ly, lz)
    ry, fy = line_parts(ny * ly, RY)
    rz, fz = line_parts(nz * lz, RZ)
    ry, fy = ry.reshape(ny, ly), fy.reshape(ny, ly)
    rz, fz = rz.reshape(nz, lz), fz.reshape(nz, lz)
    ey = np.zeros((ny, ly, lz, total))
    ez = np.zeros((nz, ly, lz, total))
    for a in range(ny):
        block = line_block(ry[a], fy[a])
        ey[a, :, :, :rows] = np.repeat(block, lz, axis=1)[:, None, :]
        ey[a, :, :, rows:far_y] = np.tile(block, (1, nz))[:, None, :]
        ey[a, :, :, far_y : far_y + lz] = fy[a][:, None, None]
        ey[a, :, :, far_y + lz : corner] = ry[a][:, None, None]
        ey[a, :, :, corner : corner + 2 * nz : 2] = fy[a][:, None, None]
        ey[a, :, :, corner + 1 : corner + 2 * nz : 2] = ry[a][:, None, None]
    for c in range(nz):
        block = line_block(rz[c], fz[c])
        ez[c, :, :, :rows] = np.tile(block, (1, ly))[None]
        ez[c, :, :, far_y:corner] = np.tile(block, (1, 2))[None]
        for b in range(nz):
            weight = fz[c] if b < c else rz[c]
            if b != c:
                ez[c, :, :, rows + b * ly : rows + (b + 1) * ly] = weight[None, :, None]
                ez[c, :, :, corner + 2 * b : corner + 2 * b + 2] = weight[None, :, None]
    coef = np.concatenate([ry.reshape(-1), fy.reshape(-1)])
    zw = np.stack([rz, fz], axis=1)[..., None] * np.ones(LANES)
    f32 = lambda t: np.asarray(t, np.float32)
    return (
        f32(coef),
        f32(zw),
        f32(ey.reshape(ny, rows, total)),
        f32(ez.reshape(nz, rows, total)),
    )


def x_tables():
    q = decay(RX)
    i = np.arange(XB)
    toep = q ** np.abs(i[:, None] - i[None, :]) * q / (RX * (1.0 - q * q))
    toep = np.asarray(toep, np.float32)
    hi = toep.astype(jnp.bfloat16)
    lo = (toep - hi.astype(np.float32)).astype(jnp.bfloat16)
    uw = np.stack([q ** (i + 1.0), q ** (XB - i * 1.0)])[:, None, :] * np.ones((1, 8, 1))
    return np.stack([hi, lo]), np.asarray(uw, np.float32)


def split(x):
    hi = x.astype(jnp.bfloat16)
    return hi, (x - hi.astype(jnp.float32)).astype(jnp.bfloat16)


def dot(a, b):
    return jnp.dot(a, b, preferred_element_type=jnp.float32)


def dot3(a, b):
    return dot(a[0], b[0]) + (dot(a[1], b[0]) + dot(a[0], b[1]))


def dot_left(parts, x):
    hi, lo = split(x)
    return dot(parts, jnp.concatenate([hi, hi, lo], axis=0))


def left_parts(w):
    hi, lo = split(w)
    return jnp.concatenate([hi, lo, hi], axis=1)


def solve_x(pieces, toeplitz):
    blocks = len(pieces)
    rows = pieces[0].shape[0]
    hi, lo = split(jnp.concatenate(pieces, axis=0))
    local = dot(hi, toeplitz[0]) + (dot(lo, toeplitz[0]) + dot(hi, toeplitz[1]))
    return [local[a * rows : (a + 1) * rows] for a in range(blocks)]


def carries(heads, tails):
    blocks = len(heads)
    q = decay(RX)
    step = float(q**XB)
    nx = blocks * XB
    head, tail = heads[-1], tails[0]
    for a in range(1, blocks):
        tail = step * tail + tails[a]
        head = step * head + heads[blocks - 1 - a]
    scale = 1.0 / (1.0 - q ** (2.0 * nx + 2.0))
    near, far = float(-q * scale), float(q ** (nx + 2.0) * scale)
    ahead = [near * head + far * tail]
    after = [near * tail + far * head]
    for a in range(blocks - 1):
        ahead.append(step * ahead[-1] + tails[a])
        after.append(step * after[-1] + heads[blocks - 1 - a])
    return ahead, after[::-1]


def along_x(pieces, toeplitz, grow, fade):
    local = solve_x(pieces, toeplitz)
    ahead, after = carries([p[:, 0:1] for p in local], [p[:, XB - 1 : XB] for p in local])
    return [p + f * grow + g * fade for p, f, g in zip(local, ahead, after)]


def kernel(
    ny, nz, owners,
    heat, speed, coef_hbm, zw_hbm, ey_hbm, ez_hbm, toep_hbm, uw_hbm,
    out,
    field, vel, zsend, zhalo, data, far_z, far_y, corner_rows, mixed,
    yface, zface, held, back, cface, chold, coef, zw, ey, ez, toep, uw,
    load_sem, hs_send, hs_recv, a_send, a_recv, b_send, b_recv, z_send, z_recv, c_send, c_recv,
):
    ly, lz, nx = heat.shape
    rows, off_y, off_c, total = sizes(ny, nz, ly, lz)
    cw = nx // owners
    half = owners // 2
    blocks = nx // XB
    my = lax.axis_index("gy")
    mz = lax.axis_index("gz")
    inner = pl.ds(LANES, nx)

    loads = [
        pltpu.make_async_copy(heat, field.at[pl.ds(1, ly), :, inner], load_sem.at[0]),
        pltpu.make_async_copy(speed, vel, load_sem.at[1]),
        pltpu.make_async_copy(coef_hbm, coef, load_sem.at[2]),
        pltpu.make_async_copy(zw_hbm, zw, load_sem.at[3]),
        pltpu.make_async_copy(ey_hbm.at[my], ey, load_sem.at[4]),
        pltpu.make_async_copy(ez_hbm.at[mz], ez, load_sem.at[5]),
        pltpu.make_async_copy(toep_hbm, toep, load_sem.at[6]),
        pltpu.make_async_copy(uw_hbm, uw, load_sem.at[7]),
    ]
    loads[0].start()

    barrier = pltpu.get_barrier_semaphore()
    for d in range(1, ny):
        pl.semaphore_signal(barrier, 1, device_id={"gy": lax.rem(my + d, ny)}, device_id_type=MESH)
    for d in range(1, nz):
        pl.semaphore_signal(barrier, 1, device_id={"gz": lax.rem(mz + d, nz)}, device_id_type=MESH)
    for load in loads[1:]:
        load.start()

    first_y, last_y = my == 0, my == ny - 1
    first_z, last_z = mz == 0, mz == nz - 1
    edge = jnp.zeros((ly + 2, lz, LANES), jnp.float32)
    field[:, :, 0:LANES] = edge
    field[:, :, LANES + nx : 2 * LANES + nx] = edge

    @pl.when(first_y)
    def _():
        field[0, :, inner] = jnp.zeros((lz, nx), jnp.float32)

    @pl.when(last_y)
    def _():
        field[ly + 1, :, inner] = jnp.zeros((lz, nx), jnp.float32)

    @pl.when(first_z)
    def _():
        zhalo[0] = jnp.zeros((ly, nx), jnp.float32)

    @pl.when(last_z)
    def _():
        zhalo[1] = jnp.zeros((ly, nx), jnp.float32)

    far_z[pl.ds(pl.multiple_of(mz * ly, 8), ly), :] = jnp.zeros((ly, nx), jnp.float32)
    corner_rows[...] = jnp.zeros_like(corner_rows)
    chold[mz] = jnp.zeros((1, 2 * nx), jnp.float32)

    loads[0].wait()
    for y in range(ly):
        zsend[0, y : y + 1, :] = field[y + 1, 0:1, inner]
        zsend[1, y : y + 1, :] = field[y + 1, lz - 1 : lz, inner]
    pl.semaphore_wait(barrier, ny - 1 + nz - 1)

    def remote(src, dst, send, recv, target):
        return pltpu.make_async_remote_copy(
            src_ref=src, dst_ref=dst, send_sem=send, recv_sem=recv,
            device_id=target, device_id_type=MESH,
        )

    down_y = lax.rem(my + ny - 1, ny)
    up_y = lax.rem(my + 1, ny)
    down_z = lax.rem(mz + nz - 1, nz)
    up_z = lax.rem(mz + 1, nz)
    y_down = remote(
        field.at[1, :, inner], field.at[ly + 1, :, inner],
        hs_send.at[0], hs_recv.at[0], {"gy": down_y},
    )
    y_up = remote(
        field.at[ly, :, inner], field.at[0, :, inner],
        hs_send.at[1], hs_recv.at[1], {"gy": up_y},
    )
    z_down = remote(zsend.at[0], zhalo.at[1], hs_send.at[2], hs_recv.at[2], {"gz": down_z})
    z_up = remote(zsend.at[1], zhalo.at[0], hs_send.at[3], hs_recv.at[3], {"gz": up_z})
    has_below = (
        (jnp.logical_not(first_y), y_down, y_up), (jnp.logical_not(first_z), z_down, z_up)
    )
    has_above = ((jnp.logical_not(last_y), y_up, y_down), (jnp.logical_not(last_z), z_up, z_down))
    ends = has_below + has_above
    for there, sent, _ in ends:
        pl.when(there)(lambda sent=sent: sent.start())

    for load in loads[1:]:
        load.wait()
    weights = ey[...] * ez[...]
    w_own = split(weights[:, :rows])
    w_z = left_parts(weights[:, rows:off_y])
    w_y = left_parts(weights[:, off_y:off_c])
    w_c = left_parts(weights[:, off_c:total])
    toeplitz = (toep[0], toep[1])
    grow, fade = uw[0, 0:1, :], uw[1, 0:1, :]

    for there, _, received in ends:
        pl.when(there)(lambda received=received: received.wait_recv())

    def column(owner):
        if owners % 2 or owners == 1:
            return pl.multiple_of(owner * cw, LANES)
        block = jnp.where(owner < half, 2 * owner, 2 * (owners - 1 - owner) + 1)
        return pl.multiple_of(block * cw, LANES)

    def owner_of(block):
        if owners % 2 or owners == 1:
            return block
        return block // 2 if block % 2 == 0 else owners - 1 - block // 2

    def to_owner(owner):
        return remote(
            yface.at[:, pl.ds(column(owner), cw)], held.at[my],
            a_send.at[owner], a_recv.at[my], {"gy": owner},
        )

    def from_peer(peer):
        return remote(
            yface.at[:, pl.ds(0, cw)], held.at[peer], a_send.at[0], a_recv.at[peer], {"gy": peer}
        )

    def owned(index, body):
        if owners == ny:
            body()
        else:
            pl.when(index < owners)(body)

    chunk = 512
    tile = lambda w: jnp.concatenate([w] * (chunk // LANES), axis=1)
    rise_z = tile(zw[mz, 0])
    fall_z = tile(zw[mz, 1])
    level = lax.broadcasted_iota(jnp.int32, (lz, chunk), 0)
    wide = chunk + 2 * LANES

    for x in range(0, nx, chunk):
        cols = pl.ds(x, chunk)
        mid = pl.ds(x + LANES, chunk)

        def layer(y, sums, x=x, cols=cols, mid=mid):
            window = field[y + 1, :, pl.ds(x, wide)]
            here = window[:, LANES : LANES + chunk]
            east = pltpu.roll(window, wide - 1, 1)[:, LANES : LANES + chunk]
            west = pltpu.roll(window, 1, 1)[:, LANES : LANES + chunk]
            south, north = field[y, :, mid], field[y + 2, :, mid]
            row = pl.ds(y, 1)
            above = jnp.where(level == lz - 1, zhalo[1, row, cols], pltpu.roll(here, lz - 1, 0))
            below = jnp.where(level == 0, zhalo[0, row, cols], pltpu.roll(here, 1, 0))
            spread = (east + west) + (north + south) + (above + below)
            moved = (
                vel[0, y, :, cols].astype(jnp.float32) * (east - west)
                + vel[1, y, :, cols].astype(jnp.float32) * (north - south)
                + vel[2, y, :, cols].astype(jnp.float32) * (above - below)
            )
            source = (1.0 - 6.0 * KAPPA) * here + KAPPA * spread - 0.5 * moved
            data[pl.ds(pl.multiple_of(y * lz, lz), lz), cols] = source
            zface[0, row, cols] = jnp.sum(source * rise_z, axis=0, keepdims=True)
            zface[1, row, cols] = jnp.sum(source * fall_z, axis=0, keepdims=True)
            place = my * ly + y
            return (sums[0] + coef[place] * source, sums[1] + coef[ny * ly + place] * source)

        zero = jnp.zeros((lz, chunk), jnp.float32)
        rising, falling = lax.fori_loop(0, ly, layer, (zero, zero), unroll=4)
        yface[0:lz, cols] = rising
        yface[lz : 2 * lz, cols] = falling
        for block in range(x // cw, (x + chunk) // cw):
            owner = owner_of(block)
            pl.when(my != owner)(lambda owner=owner: to_owner(owner).start())

    z_copies = []
    for d in range(1, nz):
        peer = lax.rem(mz + d, nz)
        side = (mz + d) // nz
        slot = far_z.at[pl.ds(pl.multiple_of(mz * ly, 8), ly)]
        copy = remote(zface.at[side], slot, z_send.at[peer], z_recv.at[mz], {"gz": peer})
        copy.start()
        z_copies.append(copy)

    parts = [slice(a * XB, (a + 1) * XB) for a in range(blocks)]
    for part in parts:
        mixed[:, part] = dot3(w_own, split(data[:, part]))

    def to_peer(peer):
        return remote(
            back.at[peer], far_y.at[:, pl.ds(column(my), cw)],
            b_send.at[peer], b_recv.at[my], {"gy": peer},
        )

    def from_owner(owner):
        return remote(
            back.at[0], far_y.at[:, pl.ds(column(owner), cw)],
            b_send.at[0], b_recv.at[owner], {"gy": owner},
        )

    def gather_sums():
        held[my] = yface[:, pl.ds(column(my), cw)]
        for d in range(1, ny):
            from_peer(lax.rem(my + d, ny)).wait_recv()
        run = jnp.zeros((lz, cw), jnp.float32)
        for a in range(ny):
            back[a, 0:lz, :] = run
            run = run + held[a, 0:lz, :]
        run = jnp.zeros((lz, cw), jnp.float32)
        for a in reversed(range(ny)):
            back[a, lz : 2 * lz, :] = run
            run = run + held[a, lz : 2 * lz, :]
        for d in range(1, ny):
            to_peer(lax.rem(my + d, ny)).start()
        far_y[:, pl.ds(column(my), cw)] = back[my]

    owned(my, gather_sums)

    for d in range(1, nz):
        peer = lax.rem(mz + d, nz)
        slot = far_z.at[pl.ds(pl.multiple_of(peer * ly, 8), ly)]
        remote(zface.at[0], slot, z_send.at[0], z_recv.at[peer], {"gz": peer}).wait_recv()
    heads, tails = [], []
    for part in parts:
        both = mixed[:, part] + dot_left(w_z, far_z[:, part])
        local = dot3(split(both), toeplitz)
        out[:, part] = local
        heads.append(local[:, 0:1])
        tails.append(local[:, XB - 1 : XB])
    ahead, after = carries(heads, tails)
    for part, f, g in zip(parts, ahead, after):
        out[:, part] += f * grow + g * fade

    for d in range(1, ny):
        owner = lax.rem(my + d, ny)
        owned(owner, lambda owner=owner: from_owner(owner).wait_recv())

    whole = lambda w: jnp.concatenate([w] * (nx // LANES), axis=1)
    for side in range(2):
        weight = whole(zw[mz, side])
        for k in range(2):
            far = far_y[k * lz : (k + 1) * lz, :]
            cface[side, :, k * nx : (k + 1) * nx] = jnp.sum(far * weight, axis=0, keepdims=True)
    c_copies = []
    for d in range(1, nz):
        peer = lax.rem(mz + d, nz)
        side = (mz + d) // nz
        copy = remote(cface.at[side], chold.at[mz], c_send.at[peer], c_recv.at[mz], {"gz": peer})
        copy.start()
        c_copies.append(copy)

    solved = along_x([far_y[:, part] for part in parts], toeplitz, grow, fade)
    for part, piece in zip(parts, solved):
        out[:, part] += dot_left(w_y, piece)

    for d in range(1, nz):
        peer = lax.rem(mz + d, nz)
        remote(
            cface.at[0], chold.at[peer], c_send.at[0], c_recv.at[peer], {"gz": peer}
        ).wait_recv()
    for b in range(nz):
        for k in range(2):
            corner_rows[2 * b + k : 2 * b + k + 1, :] = chold[b, :, k * nx : (k + 1) * nx]
    solved = along_x([corner_rows[:, part] for part in parts], toeplitz, grow, fade)
    for part, piece in zip(parts, solved):
        out[:, part] += dot_left(w_c, piece)

    for there, sent, _ in ends:
        pl.when(there)(lambda sent=sent: sent.wait_send())
    for block in range(owners):
        owner = owner_of(block)
        pl.when(my != owner)(lambda owner=owner: to_owner(owner).wait_send())
    for copy in z_copies + c_copies:
        copy.wait_send()

    def sums_sent():
        for d in range(1, ny):
            to_peer(lax.rem(my + d, ny)).wait_send()

    owned(my, sums_sent)


def on_device(ny, nz, heat, speed):
    ly, lz, nx = heat.shape
    rows, far_y, corner, total = sizes(ny, nz, ly, lz)
    owners = min(ny, nx // LANES)
    while (nx // LANES) % owners:
        owners -= 1
    cw = nx // owners
    coef, zw, ey, ez = tables(ny, nz, ly, lz)
    toep, uw = x_tables()
    hbm = pl.BlockSpec(memory_space=pltpu.HBM)
    vmem = pl.BlockSpec(memory_space=pltpu.VMEM)
    dma = pltpu.SemaphoreType.DMA
    f32 = jnp.float32
    out = pl.pallas_call(
        functools.partial(kernel, ny, nz, owners),
        out_shape=jax.ShapeDtypeStruct((rows, nx), f32),
        in_specs=[hbm] * 8,
        out_specs=vmem,
        scratch_shapes=[
            pltpu.VMEM((ly + 2, lz, nx + 2 * LANES), f32),
            pltpu.VMEM(speed.shape, speed.dtype),
            pltpu.VMEM((2, ly, nx), f32),
            pltpu.VMEM((2, ly, nx), f32),
            pltpu.VMEM((rows, nx), f32),
            pltpu.VMEM((nz * ly, nx), f32),
            pltpu.VMEM((2 * lz, nx), f32),
            pltpu.VMEM((total - corner, nx), f32),
            pltpu.VMEM((rows, nx), f32),
            pltpu.VMEM((2 * lz, nx), f32),
            pltpu.VMEM((2, ly, nx), f32),
            pltpu.VMEM((ny, 2 * lz, cw), f32),
            pltpu.VMEM((ny, 2 * lz, cw), f32),
            pltpu.VMEM((2, 1, 2 * nx), f32),
            pltpu.VMEM((nz, 1, 2 * nx), f32),
            pltpu.SMEM(coef.shape, f32),
            pltpu.VMEM(zw.shape, f32),
            pltpu.VMEM((rows, total), f32),
            pltpu.VMEM((rows, total), f32),
            pltpu.VMEM(toep.shape, jnp.bfloat16),
            pltpu.VMEM(uw.shape, f32),
            dma((8,)), dma((4,)), dma((4,)),
            dma((ny,)), dma((ny,)), dma((ny,)), dma((ny,)),
            dma((nz,)), dma((nz,)), dma((nz,)), dma((nz,)),
        ],
        compiler_params=pltpu.CompilerParams(
            collective_id=0, has_side_effects=True, vmem_limit_bytes=40 * 1024 * 1024
        ),
    )(heat, speed, jnp.asarray(coef), jnp.asarray(zw), jnp.asarray(ey), jnp.asarray(ez),
      jnp.asarray(toep), jnp.asarray(uw))
    return out.reshape(ly, lz, nx)


def solution(mesh):
    in_specs = (P("gy", "gz", None), P(None, "gy", "gz", None))
    return jax.shard_map(
        functools.partial(on_device, mesh.shape["gy"], mesh.shape["gz"]),
        mesh=mesh, in_specs=in_specs, out_specs=P("gy", "gz", None), check_vma=False,
    )
```

time: 37.7 us -> 35.1 us (0.931)
  Pallas kernels: 28.3 us -> 25.7 us
    pallas_call x1, Pallas kernels: 28.3 us -> 25.7 us  [on_device(): pl.pallas_call(functools.partial(kernel, ny, nz, owners), out_shape=jax.S...]
where the time goes in v2:
time: 35.1 us; the launch traced here: 34.6 us
  Pallas kernels  25.7 us (73%)
  local copies, waits for them, and re-layouts  8.97 us (26%)
    pallas_call x1, Pallas kernels, on_device(): pl.pallas_call(functools.partial(kernel, ny, nz, owners), out_shape=jax.S...  25.7 us
    unnamed x17, local copies, waits for them, and re-layouts  8.97 us

profile of v2, /device:TPU:0, one launch (start us, length us, event | category | flops | bytes accessed | tf_op | source)
XLA Modules:
  0.0 34.6 jit_solution(3873957637368140331)
XLA Ops:
  0.0 0.0 copy-start
  0.0 1.4 %copy-done = bf16[3,16,8,2048]{3,2,1,0:T(8,128)(2,1)S(1)} copy-done((bf16[3,16,8,2048]{3,2,1,0:T(8,128)(2,1)S(1)}, bf16[3,16,8,2048]{3,2,1,0:T(8,128)(2,1)}, u32[]{:S(2)}) %copy-start) | copy-done | bytes 1572888
  1.4 0.0 copy-start.1
  1.4 1.2 %copy-done.1 = f32[16,8,2048]{2,1,0:T(8,128)S(1)} copy-done((f32[16,8,2048]{2,1,0:T(8,128)S(1)}, f32[16,8,2048]{2,1,0:T(8,128)}, u32[]{:S(2)}) %copy-start.1) | copy-done | bytes 1048600
  2.6 0.0 copy-start.2
  2.6 1.2 %copy-done.2 = f32[8,128,224]{2,1,0:T(8,128)S(1)} copy-done((f32[8,128,224]{2,1,0:T(8,128)S(1)}, f32[8,128,224]{2,1,0:T(8,128)}, u32[]{:S(2)}) %copy-start.2) | copy-done | bytes 917528
  3.9 0.0 copy-start.3
  3.9 1.0 %copy-done.3 = f32[4,128,224]{2,1,0:T(8,128)S(1)} copy-done((f32[4,128,224]{2,1,0:T(8,128)S(1)}, f32[4,128,224]{2,1,0:T(8,128)}, u32[]{:S(2)}) %copy-start.3) | copy-done | bytes 458776
  4.9 0.0 copy-start.4
  4.9 0.9 %copy-done.4 = bf16[2,256,256]{2,1,0:T(8,128)(2,1)S(1)} copy-done((bf16[2,256,256]{2,1,0:T(8,128)(2,1)S(1)}, bf16[2,256,256]{2,1,0:T(8,128)(2,1)}, u32[]{:S(2)}) %copy-start.4) | copy-done | bytes 262168
  5.9 0.0 copy-start.5
  5.9 0.8 %copy-done.5 = f32[4,2,8,128]{3,2,1,0:T(8,128)S(1)} copy-done((f32[4,2,8,128]{3,2,1,0:T(8,128)S(1)}, f32[4,2,8,128]{3,2,1,0:T(8,128)}, u32[]{:S(2)}) %copy-start.5) | copy-done | bytes 32792
  6.6 0.0 copy-start.6
  6.6 0.7 %copy-done.6 = f32[2,8,256]{2,1,0:T(8,128)S(1)} copy-done((f32[2,8,256]{2,1,0:T(8,128)S(1)}, f32[2,8,256]{2,1,0:T(8,128)}, u32[]{:S(2)}) %copy-start.6) | copy-done | bytes 16408
  7.3 0.0 copy-start.7
  7.3 0.7 %copy-done.7 = f32[256]{0:T(256)S(1)} copy-done((f32[256]{0:T(256)S(1)}, f32[256]{0:T(256)}, u32[]{:S(2)}) %copy-start.7) | copy-done | bytes 1048
  8.0 25.7 %shard_map.82 = f32[128,2048]{1,0:T(8,128)S(1)} custom-call(f32[16,8,2048]{2,1,0:T(8,128)S(1)} %copy-done.1, bf16[3,16,8,2048]{3,2,1,0:T(8,128)(2,1)S(1)} %copy-done, f32[256]{0:T(256)S(1)} %copy-done.7, f32[4,2,8,128]{3,2,1,0:T(8,128)S(1)} %copy-done.5, f32[8,128,224]{2,1,0:T(8,128)S(1)} %copy-done.2, f32[4,128,224]{2,1,0:T(8,128)S(1)} %copy-done.3, ...), custom_call_target="tpu_custom_call" | custom-call | tf_op jit(solution)/shard_map/pallas_call | solution.py:452
  33.7 1.0 %copy.10 = f32[16,8,2048]{2,1,0:T(8,128)} copy(f32[16,8,2048]{2,1,0:T(8,128)S(1)} %bitcast.1) | data formatting | bytes 2097152
Async XLA Ops:
  0.0 1.4 %copy-start = (bf16[3,16,8,2048]{3,2,1,0:T(8,128)(2,1)S(1)}, bf16[3,16,8,2048]{3,2,1,0:T(8,128)(2,1)}, u32[]{:S(2)}) copy-start(bf16[3,16,8,2048]{3,2,1,0:T(8,128)(2,1)} %speed.1) | copy-start | bytes 4718596
  1.4 1.2 %copy-start.1 = (f32[16,8,2048]{2,1,0:T(8,128)S(1)}, f32[16,8,2048]{2,1,0:T(8,128)}, u32[]{:S(2)}) copy-start(f32[16,8,2048]{2,1,0:T(8,128)} %heat.1) | copy-start | bytes 3145732
  2.6 1.2 %copy-start.2 = (f32[8,128,224]{2,1,0:T(8,128)S(1)}, f32[8,128,224]{2,1,0:T(8,128)}, u32[]{:S(2)}) copy-start(f32[8,128,224]{2,1,0:T(8,128)} %constant.14.clone.ey_hbm) | copy-start | bytes 2752516
  3.9 1.0 %copy-start.3 = (f32[4,128,224]{2,1,0:T(8,128)S(1)}, f32[4,128,224]{2,1,0:T(8,128)}, u32[]{:S(2)}) copy-start(f32[4,128,224]{2,1,0:T(8,128)} %constant.15.clone.ez_hbm) | copy-start | bytes 1376260
  4.9 0.9 %copy-start.4 = (bf16[2,256,256]{2,1,0:T(8,128)(2,1)S(1)}, bf16[2,256,256]{2,1,0:T(8,128)(2,1)}, u32[]{:S(2)}) copy-start(bf16[2,256,256]{2,1,0:T(8,128)(2,1)} %constant.16.clone.toep_hbm) | copy-start | bytes 786436
  5.9 0.8 %copy-start.5 = (f32[4,2,8,128]{3,2,1,0:T(8,128)S(1)}, f32[4,2,8,128]{3,2,1,0:T(8,128)}, u32[]{:S(2)}) copy-start(f32[4,2,8,128]{3,2,1,0:T(8,128)} %constant.13.clone.zw_hbm) | copy-start | bytes 98308
  6.6 0.7 %copy-start.6 = (f32[2,8,256]{2,1,0:T(8,128)S(1)}, f32[2,8,256]{2,1,0:T(8,128)}, u32[]{:S(2)}) copy-start(f32[2,8,256]{2,1,0:T(8,128)} %constant.17.clone.uw_hbm) | copy-start | bytes 49156
  7.3 0.7 %copy-start.7 = (f32[256]{0:T(256)S(1)}, f32[256]{0:T(256)}, u32[]{:S(2)}) copy-start(f32[256]{0:T(256)} %constant.12.clone.coef_hbm) | copy-start | bytes 3076

commit v3 on v2

--- a/solution.py
+++ b/solution.py
@@ -154,9 +154,9 @@
     ny, nz, owners,
     heat, speed, coef_hbm, zw_hbm, ey_hbm, ez_hbm, toep_hbm, uw_hbm,
     out,
-    field, vel, zsend, zhalo, data, far_z, far_y, corner_rows, mixed,
+    field, vel, zsend, zhalo, data, far_z, far_y, corner_rows, mixed, acc,
     yface, zface, held, back, cface, chold, coef, zw, ey, ez, toep, uw,
-    load_sem, hs_send, hs_recv, a_send, a_recv, b_send, b_recv, z_send, z_recv, c_send, c_recv,
+    load_sem, out_sem, hs_send, hs_recv, a_send, a_recv, b_send, b_recv, z_send, z_recv, c_send, c_recv,
 ):
     ly, lz, nx = heat.shape
     rows, off_y, off_c, total = sizes(ny, nz, ly, lz)
@@ -229,23 +229,39 @@
     up_y = lax.rem(my + 1, ny)
     down_z = lax.rem(mz + nz - 1, nz)
     up_z = lax.rem(mz + 1, nz)
-    y_down = remote(
-        field.at[1, :, inner], field.at[ly + 1, :, inner],
-        hs_send.at[0], hs_recv.at[0], {"gy": down_y},
+    chunk = 512
+    chunks = nx // chunk
+    inside = (
+        (jnp.logical_not(first_y), jnp.logical_not(last_y)),
+        (jnp.logical_not(first_z), jnp.logical_not(last_z)),
     )
-    y_up = remote(
-        field.at[ly, :, inner], field.at[0, :, inner],
-        hs_send.at[1], hs_recv.at[1], {"gy": up_y},
-    )
-    z_down = remote(zsend.at[0], zhalo.at[1], hs_send.at[2], hs_recv.at[2], {"gz": down_z})
-    z_up = remote(zsend.at[1], zhalo.at[0], hs_send.at[3], hs_recv.at[3], {"gz": up_z})
-    has_below = (
-        (jnp.logical_not(first_y), y_down, y_up), (jnp.logical_not(first_z), z_down, z_up)
-    )
-    has_above = ((jnp.logical_not(last_y), y_up, y_down), (jnp.logical_not(last_z), z_up, z_down))
-    ends = has_below + has_above
-    for there, sent, _ in ends:
-        pl.when(there)(lambda sent=sent: sent.start())
+    ends = []
+    for n in range(chunks):
+        cols = pl.ds(n * chunk, chunk)
+        mid = pl.ds(n * chunk + LANES, chunk)
+        y_down = remote(
+            field.at[1, :, mid], field.at[ly + 1, :, mid],
+            hs_send.at[0, n], hs_recv.at[0, n], {"gy": down_y},
+        )
+        y_up = remote(
+            field.at[ly, :, mid], field.at[0, :, mid],
+            hs_send.at[1, n], hs_recv.at[1, n], {"gy": up_y},
+        )
+        z_down = remote(
+            zsend.at[0, :, cols], zhalo.at[1, :, cols],
+            hs_send.at[2, n], hs_recv.at[2, n], {"gz": down_z},
+        )
+        z_up = remote(
+            zsend.at[1, :, cols], zhalo.at[0, :, cols],
+            hs_send.at[3, n], hs_recv.at[3, n], {"gz": up_z},
+        )
+        ends.append((
+            (inside[0][0], y_down, y_up), (inside[0][1], y_up, y_down),
+            (inside[1][0], z_down, z_up), (inside[1][1], z_up, z_down),
+        ))
+    for end in ends:
+        for there, sent, _ in end:
+            pl.when(there)(lambda sent=sent: sent.start())
 
     for load in loads[1:]:
         load.wait()
@@ -257,9 +273,6 @@
     toeplitz = (toep[0], toep[1])
     grow, fade = uw[0, 0:1, :], uw[1, 0:1, :]
 
-    for there, _, received in ends:
-        pl.when(there)(lambda received=received: received.wait_recv())
-
     def column(owner):
         if owners % 2 or owners == 1:
             return pl.multiple_of(owner * cw, LANES)
@@ -288,14 +301,16 @@
         else:
             pl.when(index < owners)(body)
 
-    chunk = 512
     tile = lambda w: jnp.concatenate([w] * (chunk // LANES), axis=1)
     rise_z = tile(zw[mz, 0])
     fall_z = tile(zw[mz, 1])
     level = lax.broadcasted_iota(jnp.int32, (lz, chunk), 0)
     wide = chunk + 2 * LANES
 
+    z_copies = []
     for x in range(0, nx, chunk):
+        for there, _, received in ends[x // chunk]:
+            pl.when(there)(lambda received=received: received.wait_recv())
         cols = pl.ds(x, chunk)
         mid = pl.ds(x + LANES, chunk)
 
@@ -329,14 +344,16 @@
             owner = owner_of(block)
             pl.when(my != owner)(lambda owner=owner: to_owner(owner).start())
 
-    z_copies = []
-    for d in range(1, nz):
-        peer = lax.rem(mz + d, nz)
-        side = (mz + d) // nz
-        slot = far_z.at[pl.ds(pl.multiple_of(mz * ly, 8), ly)]
-        copy = remote(zface.at[side], slot, z_send.at[peer], z_recv.at[mz], {"gz": peer})
-        copy.start()
-        z_copies.append(copy)
+        for d in range(1, nz):
+            peer = lax.rem(mz + d, nz)
+            side = (mz + d) // nz
+            slot = far_z.at[pl.ds(pl.multiple_of(mz * ly, 8), ly), cols]
+            n = x // chunk
+            copy = remote(
+                zface.at[side, :, cols], slot, z_send.at[peer, n], z_recv.at[mz, n], {"gz": peer}
+            )
+            copy.start()
+            z_copies.append(copy)
 
     parts = [slice(a * XB, (a + 1) * XB) for a in range(blocks)]
     for part in parts:
@@ -374,18 +391,15 @@
 
     for d in range(1, nz):
         peer = lax.rem(mz + d, nz)
-        slot = far_z.at[pl.ds(pl.multiple_of(peer * ly, 8), ly)]
-        remote(zface.at[0], slot, z_send.at[0], z_recv.at[peer], {"gz": peer}).wait_recv()
-    heads, tails = [], []
-    for part in parts:
-        both = mixed[:, part] + dot_left(w_z, far_z[:, part])
-        local = dot3(split(both), toeplitz)
-        out[:, part] = local
-        heads.append(local[:, 0:1])
-        tails.append(local[:, XB - 1 : XB])
-    ahead, after = carries(heads, tails)
-    for part, f, g in zip(parts, ahead, after):
-        out[:, part] += f * grow + g * fade
+        for n in range(chunks):
+            cols = pl.ds(n * chunk, chunk)
+            slot = far_z.at[pl.ds(pl.multiple_of(peer * ly, 8), ly), cols]
+            remote(
+                zface.at[0, :, cols], slot, z_send.at[0, n], z_recv.at[peer, n], {"gz": peer}
+            ).wait_recv()
+    both = [mixed[:, part] + dot_left(w_z, far_z[:, part]) for part in parts]
+    for part, piece in zip(parts, along_x(both, toeplitz, grow, fade)):
+        acc[:, part] = piece
 
     for d in range(1, ny):
         owner = lax.rem(my + d, ny)
@@ -407,7 +421,7 @@
 
     solved = along_x([far_y[:, part] for part in parts], toeplitz, grow, fade)
     for part, piece in zip(parts, solved):
-        out[:, part] += dot_left(w_y, piece)
+        acc[:, part] += dot_left(w_y, piece)
 
     for d in range(1, nz):
         peer = lax.rem(mz + d, nz)
@@ -418,11 +432,16 @@
         for k in range(2):
             corner_rows[2 * b + k : 2 * b + k + 1, :] = chold[b, :, k * nx : (k + 1) * nx]
     solved = along_x([corner_rows[:, part] for part in parts], toeplitz, grow, fade)
-    for part, piece in zip(parts, solved):
-        out[:, part] += dot_left(w_c, piece)
-
-    for there, sent, _ in ends:
-        pl.when(there)(lambda sent=sent: sent.wait_send())
+    stores = []
+    for a, (part, piece) in enumerate(zip(parts, solved)):
+        acc[:, part] += dot_left(w_c, piece)
+        place = pl.ds(a * XB, XB)
+        stores.append(pltpu.make_async_copy(acc.at[:, place], out.at[:, place], out_sem.at[a]))
+        stores[-1].start()
+
+    for end in ends:
+        for there, sent, _ in end:
+            pl.when(there)(lambda sent=sent: sent.wait_send())
     for block in range(owners):
         owner = owner_of(block)
         pl.when(my != owner)(lambda owner=owner: to_owner(owner).wait_send())
@@ -434,6 +453,8 @@
             to_peer(lax.rem(my + d, ny)).wait_send()
 
     owned(my, sums_sent)
+    for store in stores:
+        store.wait()
 
 
 def on_device(ny, nz, heat, speed):
@@ -446,14 +467,13 @@
     coef, zw, ey, ez = tables(ny, nz, ly, lz)
     toep, uw = x_tables()
     hbm = pl.BlockSpec(memory_space=pltpu.HBM)
-    vmem = pl.BlockSpec(memory_space=pltpu.VMEM)
     dma = pltpu.SemaphoreType.DMA
     f32 = jnp.float32
     out = pl.pallas_call(
         functools.partial(kernel, ny, nz, owners),
         out_shape=jax.ShapeDtypeStruct((rows, nx), f32),
         in_specs=[hbm] * 8,
-        out_specs=vmem,
+        out_specs=hbm,
         scratch_shapes=[
             pltpu.VMEM((ly + 2, lz, nx + 2 * LANES), f32),
             pltpu.VMEM(speed.shape, speed.dtype),
@@ -463,6 +483,7 @@
             pltpu.VMEM((nz * ly, nx), f32),
             pltpu.VMEM((2 * lz, nx), f32),
             pltpu.VMEM((total - corner, nx), f32),
+            pltpu.VMEM((rows, nx), f32),
             pltpu.VMEM((rows, nx), f32),
             pltpu.VMEM((2 * lz, nx), f32),
             pltpu.VMEM((2, ly, nx), f32),
@@ -476,13 +497,11 @@
             pltpu.VMEM((rows, total), f32),
             pltpu.VMEM(toep.shape, jnp.bfloat16),
             pltpu.VMEM(uw.shape, f32),
-            dma((8,)), dma((4,)), dma((4,)),
+            dma((8,)), dma((nx // XB,)), dma((4, nx // 512)), dma((4, nx // 512)),
             dma((ny,)), dma((ny,)), dma((ny,)), dma((ny,)),
-            dma((nz,)), dma((nz,)), dma((nz,)), dma((nz,)),
+            dma((nz, nx // 512)), dma((nz, nx // 512)), dma((nz,)), dma((nz,)),
         ],
-        compiler_params=pltpu.CompilerParams(
-            collective_id=0, has_side_effects=True, vmem_limit_bytes=40 * 1024 * 1024
-        ),
+        compiler_params=pltpu.CompilerParams(collective_id=0, has_side_effects=True),
     )(heat, speed, jnp.asarray(coef), jnp.asarray(zw), jnp.asarray(ey), jnp.asarray(ez),
       jnp.asarray(toep), jnp.asarray(uw))
     return out.reshape(ly, lz, nx)

time: 35.1 us -> 28.1 us (0.80); the launches traced: 34.6 us -> 28 us
  local copies, waits for them, and re-layouts: 8.97 us -> 2.3 us
    unnamed x17 -> x1, local copies, waits for them, and re-layouts: 8.97 us -> 2.3 us
where the time goes in v3:
time: 28.1 us; the launch traced here: 28 us
  Pallas kernels  25.7 us (91%)
  local copies, waits for them, and re-layouts  2.3 us (8%)
    pallas_call x1, Pallas kernels, on_device(): pl.pallas_call(functools.partial(kernel, ny, nz, owners), out_shape=jax.S...  25.7 us
    unnamed x1, local copies, waits for them, and re-layouts  2.3 us

profile of v3, /device:TPU:0, one launch (start us, length us, event | category | flops | bytes accessed | tf_op | source)
XLA Modules:
  0.0 28.0 jit_solution(2388706475502944056)
XLA Ops:
  0.0 25.7 %shard_map.82 = f32[128,2048]{1,0:T(8,128)} custom-call(f32[16,8,2048]{2,1,0:T(8,128)} %heat.1, bf16[3,16,8,2048]{3,2,1,0:T(8,128)(2,1)} %speed.1, f32[256]{0:T(256)} %constant.12.clone.coef_hbm, f32[4,2,8,128]{3,2,1,0:T(8,128)} %constant.13.clone.zw_hbm, f32[8,128,224]{2,1,0:T(8,128)} %constant.14.clone.ey_hbm, f32[4,128,224]{2,1,0:T(8,128)} %constant.15.clone.ez_hbm, ...), custom_call_target="tpu_custom_call" | custom-call | tf_op jit(solution)/shard_map/pallas_call | solution.py:472
  25.7 2.3 %copy.10 = f32[16,8,2048]{2,1,0:T(8,128)} copy(f32[16,8,2048]{2,1,0:T(8,128)} %bitcast.1) | data formatting | bytes 2097152

commit v4 on v3

--- a/solution.py
+++ b/solution.py
@@ -153,7 +153,7 @@
 def kernel(
     ny, nz, owners,
     heat, speed, coef_hbm, zw_hbm, ey_hbm, ez_hbm, toep_hbm, uw_hbm,
-    out,
+    partial, corners,
     field, vel, zsend, zhalo, data, far_z, far_y, corner_rows, mixed, acc,
     yface, zface, held, back, cface, chold, coef, zw, ey, ez, toep, uw,
     load_sem, out_sem, hs_send, hs_recv, a_send, a_recv, b_send, b_recv, z_send, z_recv, c_send, c_recv,
@@ -269,7 +269,6 @@
     w_own = split(weights[:, :rows])
     w_z = left_parts(weights[:, rows:off_y])
     w_y = left_parts(weights[:, off_y:off_c])
-    w_c = left_parts(weights[:, off_c:total])
     toeplitz = (toep[0], toep[1])
     grow, fade = uw[0, 0:1, :], uw[1, 0:1, :]
 
@@ -420,8 +419,12 @@
         c_copies.append(copy)
 
     solved = along_x([far_y[:, part] for part in parts], toeplitz, grow, fade)
-    for part, piece in zip(parts, solved):
+    stores = []
+    for a, (part, piece) in enumerate(zip(parts, solved)):
         acc[:, part] += dot_left(w_y, piece)
+        place = pl.ds(a * XB, XB)
+        stores.append(pltpu.make_async_copy(acc.at[:, place], partial.at[:, place], out_sem.at[a]))
+        stores[-1].start()
 
     for d in range(1, nz):
         peer = lax.rem(mz + d, nz)
@@ -431,13 +434,8 @@
     for b in range(nz):
         for k in range(2):
             corner_rows[2 * b + k : 2 * b + k + 1, :] = chold[b, :, k * nx : (k + 1) * nx]
-    solved = along_x([corner_rows[:, part] for part in parts], toeplitz, grow, fade)
-    stores = []
-    for a, (part, piece) in enumerate(zip(parts, solved)):
-        acc[:, part] += dot_left(w_c, piece)
-        place = pl.ds(a * XB, XB)
-        stores.append(pltpu.make_async_copy(acc.at[:, place], out.at[:, place], out_sem.at[a]))
-        stores[-1].start()
+    stores.append(pltpu.make_async_copy(corner_rows, corners, out_sem.at[blocks]))
+    stores[-1].start()
 
     for end in ends:
         for there, sent, _ in end:
@@ -455,6 +453,45 @@
     owned(my, sums_sent)
     for store in stores:
         store.wait()
+
+
+def finish(
+    off_c, partial, corners, ey_hbm, ez_hbm, toep_hbm, uw_hbm, out,
+    acc, rows_c, ey, ez, toep, uw, load_sem, in_sem, out_sem,
+):
+    blocks = partial.shape[1] // XB
+    parts = [slice(a * XB, (a + 1) * XB) for a in range(blocks)]
+    loads = [
+        pltpu.make_async_copy(corners, rows_c, load_sem.at[0]),
+        pltpu.make_async_copy(toep_hbm, toep, load_sem.at[1]),
+        pltpu.make_async_copy(uw_hbm, uw, load_sem.at[2]),
+        pltpu.make_async_copy(ey_hbm.at[lax.axis_index("gy")], ey, load_sem.at[3]),
+        pltpu.make_async_copy(ez_hbm.at[lax.axis_index("gz")], ez, load_sem.at[4]),
+    ]
+    pieces_in, pieces_out = [], []
+    for a in range(blocks):
+        place = pl.ds(a * XB, XB)
+        pieces_in.append(
+            pltpu.make_async_copy(partial.at[:, place], acc.at[:, place], in_sem.at[a])
+        )
+        pieces_out.append(
+            pltpu.make_async_copy(acc.at[:, place], out.at[:, place], out_sem.at[a])
+        )
+    for copy in loads + pieces_in:
+        copy.start()
+    for copy in loads:
+        copy.wait()
+    w_c = left_parts(ey[:, off_c:] * ez[:, off_c:])
+    solved = along_x(
+        [rows_c[:, part] for part in parts], (toep[0], toep[1]), uw[0, 0:1, :], uw[1, 0:1, :]
+    )
+    for a, part in enumerate(parts):
+        far = dot_left(w_c, solved[a])
+        pieces_in[a].wait()
+        acc[:, part] += far
+        pieces_out[a].start()
+    for copy in pieces_out:
+        copy.wait()
 
 
 def on_device(ny, nz, heat, speed):
@@ -469,11 +506,15 @@
     hbm = pl.BlockSpec(memory_space=pltpu.HBM)
     dma = pltpu.SemaphoreType.DMA
     f32 = jnp.float32
-    out = pl.pallas_call(
+    operands = [jnp.asarray(t) for t in (coef, zw, ey, ez, toep, uw)]
+    partial, corners = pl.pallas_call(
         functools.partial(kernel, ny, nz, owners),
-        out_shape=jax.ShapeDtypeStruct((rows, nx), f32),
+        out_shape=[
+            jax.ShapeDtypeStruct((rows, nx), f32),
+            jax.ShapeDtypeStruct((total - corner, nx), f32),
+        ],
         in_specs=[hbm] * 8,
-        out_specs=hbm,
+        out_specs=[hbm] * 2,
         scratch_shapes=[
             pltpu.VMEM((ly + 2, lz, nx + 2 * LANES), f32),
             pltpu.VMEM(speed.shape, speed.dtype),
@@ -497,13 +538,27 @@
             pltpu.VMEM((rows, total), f32),
             pltpu.VMEM(toep.shape, jnp.bfloat16),
             pltpu.VMEM(uw.shape, f32),
-            dma((8,)), dma((nx // XB,)), dma((4, nx // 512)), dma((4, nx // 512)),
+            dma((8,)), dma((nx // XB + 1,)), dma((4, nx // 512)), dma((4, nx // 512)),
             dma((ny,)), dma((ny,)), dma((ny,)), dma((ny,)),
             dma((nz, nx // 512)), dma((nz, nx // 512)), dma((nz,)), dma((nz,)),
         ],
         compiler_params=pltpu.CompilerParams(collective_id=0, has_side_effects=True),
-    )(heat, speed, jnp.asarray(coef), jnp.asarray(zw), jnp.asarray(ey), jnp.asarray(ez),
-      jnp.asarray(toep), jnp.asarray(uw))
+    )(heat, speed, *operands)
+    out = pl.pallas_call(
+        functools.partial(finish, corner),
+        out_shape=jax.ShapeDtypeStruct((rows, nx), f32),
+        in_specs=[hbm] * 6,
+        out_specs=hbm,
+        scratch_shapes=[
+            pltpu.VMEM((rows, nx), f32),
+            pltpu.VMEM((total - corner, nx), f32),
+            pltpu.VMEM((rows, total), f32),
+            pltpu.VMEM((rows, total), f32),
+            pltpu.VMEM(toep.shape, jnp.bfloat16),
+            pltpu.VMEM(uw.shape, f32),
+            dma((5,)), dma((nx // XB,)), dma((nx // XB,)),
+        ],
+    )(partial, corners, *operands[2:])
     return out.reshape(ly, lz, nx)
 
 

time: 28.1 us -> 28.9 us (1.028)
  Pallas kernels: 25.7 us -> 28.8 us
  local copies, waits for them, and re-layouts: 2.3 us -> 0 us
    pallas_call x1 -> x2, Pallas kernels: 25.7 us -> 28.8 us  [the longest x1 24.8 us: on_device(): pl.pallas_call(functools.partial(kernel, ny, nz, owners), out_shape=[jax....]
    unnamed x1 -> x0, local copies, waits for them, and re-layouts: 2.3 us -> none
where the time goes in v4:
time: 28.9 us; the launch traced here: 28.8 us
  Pallas kernels  28.8 us (100%)
    pallas_call x1, Pallas kernels, on_device(): pl.pallas_call(functools.partial(kernel, ny, nz, owners), out_shape=[jax....  24.8 us
    pallas_call x1, Pallas kernels, on_device(): pl.pallas_call(functools.partial(finish, corner), out_shape=jax.ShapeDtyp...  3.98 us

profile of v4, /device:TPU:0, one launch (start us, length us, event | category | flops | bytes accessed | tf_op | source)
XLA Modules:
  0.0 28.8 jit_solution(9570176811829100524)
XLA Ops:
  0.0 24.8 %shard_map.82 = (f32[128,2048]{1,0:T(8,128)}, f32[16,2048]{1,0:T(8,128)}) custom-call(f32[16,8,2048]{2,1,0:T(8,128)} %heat.1, bf16[3,16,8,2048]{3,2,1,0:T(8,128)(2,1)} %speed.1, f32[256]{0:T(256)} %constant.12.clone.coef_hbm, f32[4,2,8,128]{3,2,1,0:T(8,128)} %constant.13.clone.zw_hbm, f32[8,128,224]{2,1,0:T(8,128)} %constant.14.clone.ey_hbm, ...), custom_call_target="tpu_custom_call" | custom-call | tf_op jit(solution)/shard_map/pallas_call | solution.py:510
  24.8 4.0 %shard_map.83 = f32[128,2048]{1,0:T(8,128)} custom-call(f32[128,2048]{1,0:T(8,128)} %get-tuple-element.7.partial, f32[16,2048]{1,0:T(8,128)} %get-tuple-element.8.corners, f32[8,128,224]{2,1,0:T(8,128)} %constant.14.clone.ey_hbm, f32[4,128,224]{2,1,0:T(8,128)} %constant.15.clone.ez_hbm, bf16[2,256,256]{2,1,0:T(8,128)(2,1)} %constant.16.clone.toep_hbm, ...), custom_call_target="tpu_custom_call" | custom-call | tf_op jit(solution)/shard_map/pallas_call | solution.py:547

commit v5 on v3

--- a/solution.py
+++ b/solution.py
@@ -152,7 +152,7 @@
 
 def kernel(
     ny, nz, owners,
-    heat, speed, coef_hbm, zw_hbm, ey_hbm, ez_hbm, toep_hbm, uw_hbm,
+    heat, speed, table,
     out,
     field, vel, zsend, zhalo, data, far_z, far_y, corner_rows, mixed, acc,
     yface, zface, held, back, cface, chold, coef, zw, ey, ez, toep, uw,
@@ -170,12 +170,21 @@
     loads = [
         pltpu.make_async_copy(heat, field.at[pl.ds(1, ly), :, inner], load_sem.at[0]),
         pltpu.make_async_copy(speed, vel, load_sem.at[1]),
-        pltpu.make_async_copy(coef_hbm, coef, load_sem.at[2]),
-        pltpu.make_async_copy(zw_hbm, zw, load_sem.at[3]),
-        pltpu.make_async_copy(ey_hbm.at[my], ey, load_sem.at[4]),
-        pltpu.make_async_copy(ez_hbm.at[mz], ez, load_sem.at[5]),
-        pltpu.make_async_copy(toep_hbm, toep, load_sem.at[6]),
-        pltpu.make_async_copy(uw_hbm, uw, load_sem.at[7]),
+        pltpu.make_async_copy(
+            table.at[ny + nz + 6 + my // 4, pl.ds(pl.multiple_of(my % 4 * 32, 32), 16)],
+            coef.at[0], load_sem.at[2],
+        ),
+        pltpu.make_async_copy(
+            table.at[ny + nz + 6 + my // 4, pl.ds(pl.multiple_of(my % 4 * 32 + 16, 16), 16)],
+            coef.at[1], load_sem.at[8],
+        ),
+        pltpu.make_async_copy(
+            table.at[ny + nz + 4, pl.ds(pl.multiple_of(mz * 16, 16), 16)], zw, load_sem.at[3]
+        ),
+        pltpu.make_async_copy(table.at[my], ey, load_sem.at[4]),
+        pltpu.make_async_copy(table.at[ny + mz], ez, load_sem.at[5]),
+        pltpu.make_async_copy(table.at[pl.ds(ny + nz, 4)], toep, load_sem.at[6]),
+        pltpu.make_async_copy(table.at[ny + nz + 5, pl.ds(0, 16)], uw, load_sem.at[7]),
     ]
     loads[0].start()
 
@@ -270,8 +279,11 @@
     w_z = left_parts(weights[:, rows:off_y])
     w_y = left_parts(weights[:, off_y:off_c])
     w_c = left_parts(weights[:, off_c:total])
-    toeplitz = (toep[0], toep[1])
-    grow, fade = uw[0, 0:1, :], uw[1, 0:1, :]
+    toeplitz = tuple(
+        jnp.concatenate([toep[2 * k, :, 0:XB], toep[2 * k + 1, :, 0:XB]], axis=0).astype(jnp.bfloat16)
+        for k in range(2)
+    )
+    grow, fade = uw[0:1, 0:XB], uw[8:9, 0:XB]
 
     def column(owner):
         if owners % 2 or owners == 1:
@@ -302,8 +314,8 @@
             pl.when(index < owners)(body)
 
     tile = lambda w: jnp.concatenate([w] * (chunk // LANES), axis=1)
-    rise_z = tile(zw[mz, 0])
-    fall_z = tile(zw[mz, 1])
+    rise_z = tile(zw[0:8, 0:LANES])
+    fall_z = tile(zw[8:16, 0:LANES])
     level = lax.broadcasted_iota(jnp.int32, (lz, chunk), 0)
     wide = chunk + 2 * LANES
 
@@ -333,8 +345,9 @@
             data[pl.ds(pl.multiple_of(y * lz, lz), lz), cols] = source
             zface[0, row, cols] = jnp.sum(source * rise_z, axis=0, keepdims=True)
             zface[1, row, cols] = jnp.sum(source * fall_z, axis=0, keepdims=True)
-            place = my * ly + y
-            return (sums[0] + coef[place] * source, sums[1] + coef[ny * ly + place] * source)
+            rise_y = jnp.concatenate([coef[0, pl.ds(y, 1), 0:XB]] * (chunk // XB), axis=1)
+            fall_y = jnp.concatenate([coef[1, pl.ds(y, 1), 0:XB]] * (chunk // XB), axis=1)
+            return (sums[0] + rise_y * source, sums[1] + fall_y * source)
 
         zero = jnp.zeros((lz, chunk), jnp.float32)
         rising, falling = lax.fori_loop(0, ly, layer, (zero, zero), unroll=4)
@@ -407,7 +420,7 @@
 
     whole = lambda w: jnp.concatenate([w] * (nx // LANES), axis=1)
     for side in range(2):
-        weight = whole(zw[mz, side])
+        weight = whole(zw[8 * side : 8 * side + 8, 0:LANES])
         for k in range(2):
             far = far_y[k * lz : (k + 1) * lz, :]
             cface[side, :, k * nx : (k + 1) * nx] = jnp.sum(far * weight, axis=0, keepdims=True)
@@ -466,13 +479,23 @@
     cw = nx // owners
     coef, zw, ey, ez = tables(ny, nz, ly, lz)
     toep, uw = x_tables()
+    wide = -(-total // XB) * XB
+    table = np.zeros((ny + nz + 6 + -(-ny // 4), rows, wide), np.float32)
+    table[:ny, :, :total] = ey
+    table[ny : ny + nz, :, :total] = ez
+    table[ny + nz : ny + nz + 4, :, :XB] = toep.astype(np.float32).reshape(4, rows, XB)
+    table[ny + nz + 4, : 16 * nz, :LANES] = zw.reshape(16 * nz, LANES)
+    table[ny + nz + 5, :16, :XB] = uw.reshape(16, XB)
+    for a in range(ny):
+        slab, row = ny + nz + 6 + a // 4, a % 4 * 32
+        table[slab, row : row + 32] = coef.reshape(2, ny, ly)[:, a].reshape(32, 1)
     hbm = pl.BlockSpec(memory_space=pltpu.HBM)
     dma = pltpu.SemaphoreType.DMA
     f32 = jnp.float32
     out = pl.pallas_call(
         functools.partial(kernel, ny, nz, owners),
         out_shape=jax.ShapeDtypeStruct((rows, nx), f32),
-        in_specs=[hbm] * 8,
+        in_specs=[hbm] * 3,
         out_specs=hbm,
         scratch_shapes=[
             pltpu.VMEM((ly + 2, lz, nx + 2 * LANES), f32),
@@ -491,19 +514,18 @@
             pltpu.VMEM((ny, 2 * lz, cw), f32),
             pltpu.VMEM((2, 1, 2 * nx), f32),
             pltpu.VMEM((nz, 1, 2 * nx), f32),
-            pltpu.SMEM(coef.shape, f32),
-            pltpu.VMEM(zw.shape, f32),
-            pltpu.VMEM((rows, total), f32),
-            pltpu.VMEM((rows, total), f32),
-            pltpu.VMEM(toep.shape, jnp.bfloat16),
-            pltpu.VMEM(uw.shape, f32),
-            dma((8,)), dma((nx // XB,)), dma((4, nx // 512)), dma((4, nx // 512)),
+            pltpu.VMEM((2, 16, wide), f32),
+            pltpu.VMEM((16, wide), f32),
+            pltpu.VMEM((rows, wide), f32),
+            pltpu.VMEM((rows, wide), f32),
+            pltpu.VMEM((4, rows, wide), f32),
+            pltpu.VMEM((16, wide), f32),
+            dma((9,)), dma((nx // XB,)), dma((4, nx // 512)), dma((4, nx // 512)),
             dma((ny,)), dma((ny,)), dma((ny,)), dma((ny,)),
             dma((nz, nx // 512)), dma((nz, nx // 512)), dma((nz,)), dma((nz,)),
         ],
-        compiler_params=pltpu.CompilerParams(collective_id=0, has_side_effects=True),
-    )(heat, speed, jnp.asarray(coef), jnp.asarray(zw), jnp.asarray(ey), jnp.asarray(ez),
-      jnp.asarray(toep), jnp.asarray(uw))
+        compiler_params=pltpu.CompilerParams(collective_id=0, has_side_effects=True, vmem_limit_bytes=53336 * 1024),
+    )(heat, speed, jnp.asarray(table))
     return out.reshape(ly, lz, nx)
 
 

time: 28.1 us -> 27.2 us (0.968)
  local copies, waits for them, and re-layouts: 2.3 us -> 0.97 us
  Pallas kernels: 25.7 us -> 26 us
    unnamed x1, local copies, waits for them, and re-layouts: 2.3 us -> 0.97 us
    pallas_call x1, Pallas kernels: 25.7 us -> 26 us  [on_device(): pl.pallas_call(functools.partial(kernel, ny, nz, owners), out_shape=jax.S...]
where the time goes in v5:
time: 27.2 us; the launch traced here: 27 us
  Pallas kernels  26 us (96%)
  local copies, waits for them, and re-layouts  0.97 us (4%)
    pallas_call x1, Pallas kernels, on_device(): pl.pallas_call(functools.partial(kernel, ny, nz, owners), out_shape=jax.S...  26 us
    unnamed x1, local copies, waits for them, and re-layouts  0.97 us

profile of v5, /device:TPU:0, one launch (start us, length us, event | category | flops | bytes accessed | tf_op | source)
XLA Modules:
  0.0 27.0 jit_solution(1484381777898409442)
XLA Ops:
  0.0 26.0 %shard_map.37 = f32[128,2048]{1,0:T(8,128)S(1)} custom-call(f32[16,8,2048]{2,1,0:T(8,128)} %heat.1, bf16[3,16,8,2048]{3,2,1,0:T(8,128)(2,1)} %speed.1, f32[20,128,256]{2,1,0:T(8,128)} %constant.2.clone.table), custom_call_target="tpu_custom_call" | custom-call | tf_op jit(solution)/shard_map/pallas_call | solution.py:495
  26.0 1.0 %copy.5 = f32[16,8,2048]{2,1,0:T(8,128)} copy(f32[16,8,2048]{2,1,0:T(8,128)S(1)} %bitcast.1) | data formatting | bytes 2097152

commit v6 on v5

--- a/solution.py
+++ b/solution.py
@@ -222,10 +222,6 @@
     corner_rows[...] = jnp.zeros_like(corner_rows)
     chold[mz] = jnp.zeros((1, 2 * nx), jnp.float32)
 
-    loads[0].wait()
-    for y in range(ly):
-        zsend[0, y : y + 1, :] = field[y + 1, 0:1, inner]
-        zsend[1, y : y + 1, :] = field[y + 1, lz - 1 : lz, inner]
     pl.semaphore_wait(barrier, ny - 1 + nz - 1)
 
     def remote(src, dst, send, recv, target):
@@ -249,11 +245,11 @@
         cols = pl.ds(n * chunk, chunk)
         mid = pl.ds(n * chunk + LANES, chunk)
         y_down = remote(
-            field.at[1, :, mid], field.at[ly + 1, :, mid],
+            heat.at[0, :, cols], field.at[ly + 1, :, mid],
             hs_send.at[0, n], hs_recv.at[0, n], {"gy": down_y},
         )
         y_up = remote(
-            field.at[ly, :, mid], field.at[0, :, mid],
+            heat.at[ly - 1, :, cols], field.at[0, :, mid],
             hs_send.at[1, n], hs_recv.at[1, n], {"gy": up_y},
         )
         z_down = remote(
@@ -269,7 +265,14 @@
             (inside[1][0], z_down, z_up), (inside[1][1], z_up, z_down),
         ))
     for end in ends:
-        for there, sent, _ in end:
+        for there, sent, _ in end[:2]:
+            pl.when(there)(lambda sent=sent: sent.start())
+    loads[0].wait()
+    for y in range(ly):
+        zsend[0, y : y + 1, :] = field[y + 1, 0:1, inner]
+        zsend[1, y : y + 1, :] = field[y + 1, lz - 1 : lz, inner]
+    for end in ends:
+        for there, sent, _ in end[2:]:
             pl.when(there)(lambda sent=sent: sent.start())
 
     for load in loads[1:]:

time: 27.2 us -> 27.2 us (level)
  no operation moved by 1% of the time
where the time goes in v6:
time: 27.2 us; the launch traced here: 27.1 us
  Pallas kernels  26.1 us (96%)
  local copies, waits for them, and re-layouts  0.97 us (4%)
    pallas_call x1, Pallas kernels, on_device(): pl.pallas_call(functools.partial(kernel, ny, nz, owners), out_shape=jax.S...  26.1 us
    unnamed x1, local copies, waits for them, and re-layouts  0.97 us

profile of v6, /device:TPU:0, one launch (start us, length us, event | category | flops | bytes accessed | tf_op | source)
XLA Modules:
  0.0 27.1 jit_solution(1836854252971301136)
XLA Ops:
  0.0 26.1 %shard_map.37 = f32[128,2048]{1,0:T(8,128)S(1)} custom-call(f32[16,8,2048]{2,1,0:T(8,128)} %heat.1, bf16[3,16,8,2048]{3,2,1,0:T(8,128)(2,1)} %speed.1, f32[20,128,256]{2,1,0:T(8,128)} %constant.2.clone.table), custom_call_target="tpu_custom_call" | custom-call | tf_op jit(solution)/shard_map/pallas_call | solution.py:498
  26.1 1.0 %copy.5 = f32[16,8,2048]{2,1,0:T(8,128)} copy(f32[16,8,2048]{2,1,0:T(8,128)S(1)} %bitcast.1) | data formatting | bytes 2097152
